TPU v7x, 128 devices: a whole 4x4x4 slice. The times are simulated.
128 devices in a mesh: rep: 4 (over z_hi, core), fsdp: 32 (over z_lo, x, y).
Axes of the slice: x: 4, y: 4, z: 4 (z_hi: 2, z_lo: 2; z = z_hi * 2 + z_lo), core: 2. Of those that a mesh axis runs over, the one named last changes fastest.
Arguments:
- layer_input: bfloat16 [4, 16384, 8192], P('rep', 'fsdp'), may hold values from -512 to 512
- value_weight: bfloat16 [4, 8192, 512], P('rep', 'fsdp'), may hold values from -6 to 6
- norm_gain: bfloat16 [4, 8192], P('rep', 'fsdp'), may hold values from 0.25 to 1.75
- cotangent: bfloat16 [4, 16384, 512], P('rep', 'fsdp'), may hold values from -6 to 6
- frag_global: float32 [8192, 1024], P('fsdp'), may hold values from -6 to 6
- frag_momentum: float32 [8192, 1024], P('fsdp'), may hold values from -3 to 3
- frag_snapshot: bfloat16 [4, 8192, 1024], P('rep', 'fsdp'), may hold values from -6 to 6
- frag_local: bfloat16 [4, 8192, 1024], P('rep', 'fsdp'), may hold values from -6 to 6
Outputs:
- values: bfloat16 [4, 16384, 512], P('rep', 'fsdp')
- input_grad: bfloat16 [4, 16384, 8192], P('rep', 'fsdp')
- weight_grad: float32 [4, 8192, 512], P('rep', 'fsdp')
- new_global: float32 [8192, 1024], P('fsdp')
- new_momentum: float32 [8192, 1024], P('fsdp')
- new_local: bfloat16 [4, 8192, 1024], P('rep', 'fsdp')
All inputs are finite; a program needn't handle non-finite values.
Results may differ from a plain program's by a relative error of at most 0.005.
Values may be sent and summed in bfloat16 or wider, within the bound.
No kernel may reach another device: no remote copies, remote signals or barrier semaphores. Data moves between devices by JAX's collectives and lax.ppermute only.
A program may use at most 192 MiB of HBM per device.

v0:
```python
import jax
import jax.numpy as jnp
from jax import lax
from jax.sharding import PartitionSpec as P

epsilon = 1e-05
outer_rate = 0.7
outer_beta = 0.9
merge_weight = 0.5


def body(
    layer_input,
    value_weight,
    norm_gain,
    cotangent,
    frag_global,
    frag_momentum,
    frag_snapshot,
    frag_local,
):
    tokens = layer_input[0]
    upstream = cotangent[0]
    weight_rows = value_weight[0]
    gain_rows = norm_gain[0]
    model_width = tokens.shape[1]
    factor = float(model_width) ** (-0.5)
    wide_inputs = tokens.astype(jnp.float32)
    radius = jnp.sqrt(jnp.mean(wide_inputs * wide_inputs, axis=1, keepdims=True) + epsilon)
    normed = wide_inputs / radius
    contract_last = (((1,), (1,)), ((), ()))
    weight_piece = lax.all_gather(weight_rows, "fsdp", axis=0, tiled=True)
    gain_piece = lax.all_gather(gain_rows, "fsdp", axis=0, tiled=True)
    window = normed
    scaled_piece = (window * gain_piece.astype(jnp.float32)[None, :]).astype(jnp.bfloat16)
    summed_rows = jnp.dot(scaled_piece, weight_piece, preferred_element_type=jnp.float32)
    weight_piece = lax.all_gather(weight_rows, "fsdp", axis=0, tiled=True)
    gain_piece = lax.all_gather(gain_rows, "fsdp", axis=0, tiled=True)
    partial_adjoint = (
        factor
        * lax.dot_general(upstream, weight_piece, contract_last, preferred_element_type=jnp.float32)
        * gain_piece.astype(jnp.float32)[None, :]
    )
    values = (factor * summed_rows).astype(jnp.bfloat16)
    correction = jnp.mean(partial_adjoint * normed, axis=1, keepdims=True)
    input_grad = ((partial_adjoint - normed * correction) / radius).astype(jnp.bfloat16)
    window = scaled_piece
    weight_grad = lax.psum_scatter(
        factor
        * lax.dot_general(
            window, upstream, (((0,), (0,)), ((), ())), preferred_element_type=jnp.float32
        ),
        "fsdp",
        scatter_dimension=0,
        tiled=True,
    )
    own_delta = frag_global - frag_snapshot[0].astype(jnp.float32)
    replica_count = lax.axis_size("rep")
    summed = lax.psum(own_delta, "rep")
    mean_delta = summed / replica_count
    new_momentum = outer_beta * frag_momentum + mean_delta
    new_global = frag_global - outer_rate * (mean_delta + outer_beta * new_momentum)
    new_local = (
        merge_weight * frag_local[0].astype(jnp.float32) + (1.0 - merge_weight) * new_global
    ).astype(jnp.bfloat16)
    return (
        values[None],
        input_grad[None],
        weight_grad[None],
        new_global,
        new_momentum,
        new_local[None],
    )


def solution(mesh):
    return jax.shard_map(
        body,
        mesh=mesh,
        in_specs=(
            P("rep", "fsdp", None),
            P("rep", "fsdp", None),
            P("rep", "fsdp"),
            P("rep", "fsdp", None),
            P("fsdp", None),
            P("fsdp", None),
            P("rep", "fsdp", None),
            P("rep", "fsdp", None),
        ),
        out_specs=(
            P("rep", "fsdp", None),
            P("rep", "fsdp", None),
            P("rep", "fsdp", None),
            P("fsdp", None),
            P("fsdp", None),
            P("rep", "fsdp", None),
        ),
        check_vma=False,
    )
```

profile of v0, /device:TPU:0, one launch (start us, length us, event | category | flops | bytes accessed | tf_op | source)
XLA Modules:
  0.0 398.2 jit_solution(1445705066393905426)
XLA Ops:
  8.0 0.0 copy-start
  8.0 0.0 all-reduce.2.cloned.1.call-start
  8.1 2.6 convert_subtract_fusion
  10.6 0.0 all-reduce.2.cloned.1.call-update
  10.7 0.0 all-gather.4.cloned.1.call-start
  10.7 0.5 all-gather.4.cloned.1.call-update
  11.2 0.0 reduce-scatter.2.cloned.1.call-start
  11.3 82.4 %all-gather = bf16[1,8192]{1,0:T(2,128)(2,1)S(1)} all-gather(bf16[1,256]{1,0:T(2,128)(2,1)} %param.10), channel_id=2, replica_groups=mesh['rep'=4,'fsdp'=32] {'fsdp'}, dimensions={1}, use_global_device_ids=true | all-gather | bytes 16896 | tf_op jit(solution)/shard_map/all_gather | solution.py:33
  93.7 5.1 %fusion.2 = f32[512]{0:T(512)S(1)} fusion(bf16[1,512,8192]{2,1,0:T(8,128)(2,1)} %param.8), kind=kLoop, calls=%fused_computation.4 | loop fusion | flops 12582400 | bytes 8390656 | tf_op jit(solution)/shard_map/reduce_sum | solution.py:29
  98.8 0.0 copy-done
  98.8 13.9 %convolution_multiply_fusion = f32[8192,512]{1,0:T(8,128)} fusion(bf16[1,512,8192]{2,1,0:T(8,128)(2,1)} %param.8, f32[8192]{0:T(1024)S(1)} %bitcast.54, f32[512]{0:T(512)S(1)} %add_sqrt_fusion, bf16[1,512,512]{2,1,0:T(8,128)(2,1)S(1)} %copy-done), kind=kOutput, calls=%fused_computation.10 | convolution fusion | flops 4315938816 | bytes 25724928 | tf_op jit(solution)/shard_map/dot_general | solution.py:50
  112.8 0.0 copy-start.2
  112.8 0.0 copy-start.3
  112.8 0.0 copy-start.4
  112.8 0.0 reduce-scatter.2.cloned.1.call-update
  112.8 0.0 all-reduce.2.cloned.1.call-done
  112.8 1.2 copy-done.2
  114.0 0.3 copy-done.3
  114.3 0.1 copy-done.4
  114.5 3.1 fusion.26
  117.6 65.6 %all-gather.4.cloned.1.call-done = bf16[1,8192,512]{2,1,0:T(8,128)(2,1)} async-done(((bf16[1,256,512]{2,1,0:T(8,128)(2,1)}), bf16[1,8192,512]{2,1,0:T(8,128)(2,1)}) %all-gather.4.cloned.1.call-update) | async-done | bytes 8388624 | tf_op jit(solution)/shard_map/all_gather | solution.py:32
  183.2 0.0 slice-start
  183.2 13.3 %multiply_reduce_fusion = (f32[512]{0:T(512)S(1)}, f32[512,8192]{1,0:T(8,128)}) fusion(f32[8192]{0:T(1024)S(1)} %broadcast_multiply_fusion, f32[512]{0:T(512)S(1)} %add_sqrt_fusion, bf16[1,512,8192]{2,1,0:T(8,128)(2,1)} %param.8, bf16[1,8192,512]{2,1,0:T(8,128)(2,1)} %all-gather.4.cloned.1.call-done, bf16[1,512,512]{2,1,0:T(8,128)(2,1)S(1)} %copy-done), kind=kOutput, calls=%fused_computation.8 | convolution fusion | flops 4315938304 | bytes 34115584 | tf_op jit(solution)/shard_map/dot_general | solution.py:41
  196.5 0.0 slice-start.1
  196.5 11.2 %fusion.21 = bf16[1,512,512]{2,1,0:T(8,128)(2,1)} fusion(bf16[1,8192,512]{2,1,0:T(8,128)(2,1)} %all-gather.4.cloned.1.call-done, f32[8192]{0:T(1024)S(1)} %bitcast.56, bf16[1,512,8192]{2,1,0:T(8,128)(2,1)} %param.8, f32[512]{0:T(512)S(1)} %add_sqrt_fusion), kind=kOutput, calls=%fused_computation.22 | convolution fusion | flops 4312268800 | bytes 17336320 | tf_op jit(solution)/shard_map/dot_general | solution.py:36
  207.7 0.0 copy-start.1
  207.7 0.0 slice-done
  207.8 0.0 slice-done.1
  207.8 10.6 %fusion.14 = bf16[1,512,8192]{2,1,0:T(8,128)(2,1)} fusion(f32[512]{0:T(512)S(1)} %add_sqrt_fusion, f32[512]{0:T(512)S(1)} %broadcast_multiply_fusion.1, f32[512,8192]{1,0:T(8,128)} %get-tuple-element.10, f32[8192]{0:T(1024)S(1)} %broadcast_multiply_fusion, bf16[1,512,8192]{2,1,0:T(8,128)(2,1)S(1)} %bitcast.53), kind=kLoop, calls=%fused_computation.19 | loop fusion | flops 29360128 | bytes 33591296 | tf_op jit(solution)/shard_map/broadcast_in_dim | solution.py:68
  218.4 172.4 %reduce-scatter.2.cloned.1.call-done = f32[256,512]{1,0:T(8,128)} async-done(((f32[8192,512]{1,0:T(8,128)}), f32[256,512]{1,0:T(8,128)}) %reduce-scatter.2.cloned.1.call-update) | async-done | bytes 524304 | tf_op jit(solution)/shard_map/reduce_scatter | solution.py:48
  390.7 0.0 copy-done.1
  (5 shorter events, 0.1 us)
Async XLA Ops:
  8.0 90.8 %copy-start = (bf16[1,512,512]{2,1,0:T(8,128)(2,1)S(1)}, bf16[1,512,512]{2,1,0:T(8,128)(2,1)}, u32[]{:S(2)}) copy-start(bf16[1,512,512]{2,1,0:T(8,128)(2,1)} %param.11) | copy-start | bytes 1572868
  8.0 104.8 %all-reduce.2.cloned.1.call-start = ((), (), s32[]{:S(2)}) async-start(), calls=%async_computation.2 | async-start | bytes 2097152 | tf_op jit(solution)/shard_map/psum | solution.py:59
  10.7 172.5 %all-gather.4.cloned.1.call-start = ((), (), s32[]{:S(2)}) async-start(), calls=%async_computation.3 | async-start | bytes 8650752 | tf_op jit(solution)/shard_map/all_gather | solution.py:32
  11.2 379.5 %reduce-scatter.2.cloned.1.call-start = ((), (), s32[]{:S(2)}) async-start(), calls=%async_computation.1 | async-start | bytes 17301504 | tf_op jit(solution)/shard_map/reduce_scatter | solution.py:48
  112.8 1.2 copy-start.2
  112.8 1.6 copy-start.3
  112.8 1.7 copy-start.4
  183.2 24.6 %slice-start = ((s8[8388608]{0:T(1024)(128)(4,1)}), s8[4194304]{0:T(1024)(128)(4,1)S(1)}, s32[]{:S(2)}) async-start(s8[8388608]{0:T(1024)(128)(4,1)} %bitcast.52), calls=%async_computation.4 | async-start | bytes 8388608
  196.5 11.3 %slice-start.1 = ((s8[8388608]{0:T(1024)(128)(4,1)}), s8[4194304]{0:T(1024)(128)(4,1)S(1)}, s32[]{:S(2)}) async-start(s8[8388608]{0:T(1024)(128)(4,1)} %bitcast.52), calls=%async_computation.5 | async-start | bytes 8388608
  207.7 183.0 %copy-start.1 = (bf16[1,512,512]{2,1,0:T(8,128)(2,1)S(1)}, bf16[1,512,512]{2,1,0:T(8,128)(2,1)}, u32[]{:S(2)}) copy-start(bf16[1,512,512]{2,1,0:T(8,128)(2,1)} %param.11) | copy-start | bytes 1572868
Sparse Core Ops, SparseCore 0:
  11.9 72.7 all-reduce.1
Sparse Core Ops, SparseCore 1:
  12.8 170.4 all-gather.3
  186.0 204.6 reduce-scatter.1
where the time goes:
time: 398 us
  waiting for transfers between devices  239 us (60%)
  blocking collectives  82.4 us (21%)
  matrix products  38.5 us (10%)
  other arithmetic  21.5 us (5%)
  between operations  15.5 us (4%)
    reduce_scatter x1, waiting for transfers between devices, body(): lax.psum_scatter(factor * lax.dot_general(window, upstream, (((0,), (0,))...  172 us
    all_gather x1, blocking collectives, body(): gain_piece = lax.all_gather(gain_rows, 'fsdp', axis=0, tiled=True)  82.4 us
    all_gather x1, waiting for transfers between devices, body(): weight_piece = lax.all_gather(weight_rows, 'fsdp', axis=0, tiled=True)  65.6 us
    dot_general x1, matrix products, body(): lax.dot_general(window, upstream, (((0,), (0,)), ((), ())), preferred_ele...  13.9 us
    dot_general x1, matrix products, body(): lax.dot_general(upstream, weight_piece, contract_last, preferred_element_...  13.3 us
    dot_general x1, matrix products, body(): jnp.dot(scaled_piece, weight_piece, preferred_element_type=jnp.float32)  11.2 us
    broadcast_in_dim x1, other arithmetic, body(): input_grad[None]  10.6 us
  transfers between devices with their start and end apart: 3, of which 2 were waited for; matrix products, arithmetic and copies ran while one was open for 14% of the time, Pallas kernels for 0%

commit v1 on v0

v1 whole, which is shorter than its diff:
```python
import functools

import jax
import jax.numpy as jnp
from jax import lax
from jax.experimental import pallas as pl
from jax.experimental.pallas import tpu as pltpu
from jax.sharding import PartitionSpec as P

epsilon = 1e-05
outer_rate = 0.7
outer_beta = 0.9
merge_weight = 0.5

NZ, NX, NY = 2, 4, 4
BLOCKS = NZ * NX
MIB = 1 << 20


def _index(z, x, y):
    return (z * NX + x) * NY + y


X_GROUPS = [[_index(z, x, y) for x in range(NX)] for z in range(NZ) for y in range(NY)]
Y_GROUPS = [[_index(z, x, y) for y in range(NY)] for z in range(NZ) for x in range(NX)]
ZY_GROUPS = [[_index(z, x, y) for z in range(NZ) for y in range(NY)] for x in range(NX)]
ZX_GROUPS = [[_index(z, x, y) for z in range(NZ) for x in range(NX)] for y in range(NY)]
OTHER_CORE = [(0, 1), (1, 0), (2, 3), (3, 2)]
OTHER_Z = [(0, 2), (2, 0), (1, 3), (3, 1)]


def weight_grad_kernel(width, x_ref, cot_ref, out_ref, inv_ref, held, total, scaled):
    phase, j = pl.program_id(0), pl.program_id(1)
    tokens, cols = x_ref.shape

    @pl.when(phase == 0)
    def _():
        x = x_ref[...]
        held[j] = x
        wide = x.astype(jnp.float32)
        squares = wide * wide
        part = squares[:, :128]
        for k in range(1, cols // 128):
            part = part + squares[:, k * 128 : (k + 1) * 128]

        @pl.when(j == 0)
        def _():
            total[...] = part

        @pl.when(j > 0)
        def _():
            total[...] += part

    @pl.when(phase == 1)
    def _():
        @pl.when(j == 0)
        def _():
            mean = jnp.sum(total[...], axis=1, keepdims=True) / width
            inv = 1.0 / jnp.sqrt(mean + epsilon)
            inv_ref[...] = jnp.broadcast_to(inv, inv_ref.shape)
            scaled[...] = (cot_ref[...].astype(jnp.float32) * inv).astype(jnp.bfloat16)

        rows = cols // NY
        for y in range(NY):
            out_ref[y, 0] = lax.dot_general(
                held[j, :, y * rows : (y + 1) * rows],
                scaled[...],
                (((0,), (0,)), ((), ())),
                preferred_element_type=jnp.float32,
            ).astype(jnp.bfloat16)


def weight_grad_partial(x, cot):
    tokens, width = x.shape
    kv = cot.shape[1]
    cols = width // BLOCKS
    rows = cols // NY
    return pl.pallas_call(
        functools.partial(weight_grad_kernel, width),
        grid=(2, BLOCKS),
        in_specs=[
            pl.BlockSpec((tokens, cols), lambda p, j: (0, jnp.where(p == 0, j, BLOCKS - 1))),
            pl.BlockSpec((tokens, kv), lambda p, j: (0, 0)),
        ],
        out_specs=[
            pl.BlockSpec((NY, 1, rows, kv), lambda p, j: (0, jnp.where(p == 0, 0, j), 0, 0)),
            pl.BlockSpec((tokens, 128), lambda p, j: (0, 0)),
        ],
        out_shape=[
            jax.ShapeDtypeStruct((NY, BLOCKS, rows, kv), jnp.bfloat16),
            jax.ShapeDtypeStruct((tokens, 128), jnp.float32),
        ],
        scratch_shapes=[
            pltpu.VMEM((BLOCKS, tokens, cols), jnp.bfloat16),
            pltpu.VMEM((tokens, 128), jnp.float32),
            pltpu.VMEM((tokens, kv), jnp.bfloat16),
        ],
        compiler_params=pltpu.CompilerParams(vmem_limit_bytes=32 * MIB),
        cost_estimate=pl.CostEstimate(
            flops=2 * tokens * width * kv, bytes_accessed=4 * tokens * width, transcendentals=0
        ),
        name="weight_grad_partial",
    )(x, cot)


def input_grad_kernel(width, factor, x_ref, w_ref, cot_ref, inv_ref, val_ref, out_ref, held_x, held_w, total, shift):
    phase, j = pl.program_id(0), pl.program_id(1)

    @pl.when(phase == 0)
    def _():
        held_x[j] = x_ref[...]
        held_w[j] = w_ref[0, 0]
        part = jnp.dot(x_ref[...], w_ref[0, 0], preferred_element_type=jnp.float32)

        @pl.when(j == 0)
        def _():
            total[...] = part

        @pl.when(j > 0)
        def _():
            total[...] += part

    @pl.when(phase == 1)
    def _():
        inv = inv_ref[:, :1]

        @pl.when(j == 0)
        def _():
            values = total[...] * (factor * inv)
            val_ref[...] = values.astype(jnp.bfloat16)
            mean = jnp.sum(cot_ref[...].astype(jnp.float32) * values, axis=1, keepdims=True) / width
            shift[...] = jnp.broadcast_to(mean * inv * inv, shift.shape)

        adjoint = lax.dot_general(
            cot_ref[...], held_w[j], (((1,), (1,)), ((), ())), preferred_element_type=jnp.float32
        )
        out_ref[...] = (
            adjoint * (factor * inv) - held_x[j].astype(jnp.float32) * shift[:, :1]
        ).astype(jnp.bfloat16)


def values_and_input_grad(x, w, cot, inv):
    tokens, width = x.shape
    kv = cot.shape[1]
    cols = width // BLOCKS
    factor = float(width) ** (-0.5)
    last = BLOCKS - 1
    return pl.pallas_call(
        functools.partial(input_grad_kernel, width, factor),
        grid=(2, BLOCKS),
        in_specs=[
            pl.BlockSpec((tokens, cols), lambda p, j: (0, jnp.where(p == 0, j, last))),
            pl.BlockSpec(
                (1, 1, cols, kv),
                lambda p, j: (jnp.where(p == 0, j % NX, NX - 1), jnp.where(p == 0, j // NX, NZ - 1), 0, 0),
            ),
            pl.BlockSpec((tokens, kv), lambda p, j: (0, 0)),
            pl.BlockSpec((tokens, 128), lambda p, j: (0, 0)),
        ],
        out_specs=[
            pl.BlockSpec((tokens, kv), lambda p, j: (0, 0)),
            pl.BlockSpec((tokens, cols), lambda p, j: (0, jnp.where(p == 0, 0, j))),
        ],
        out_shape=[
            jax.ShapeDtypeStruct((tokens, kv), jnp.bfloat16),
            jax.ShapeDtypeStruct((tokens, width), jnp.bfloat16),
        ],
        scratch_shapes=[
            pltpu.VMEM((BLOCKS, tokens, cols), jnp.bfloat16),
            pltpu.VMEM((BLOCKS, cols, kv), jnp.bfloat16),
            pltpu.VMEM((tokens, kv), jnp.float32),
            pltpu.VMEM((tokens, 128), jnp.float32),
        ],
        compiler_params=pltpu.CompilerParams(vmem_limit_bytes=40 * MIB),
        cost_estimate=pl.CostEstimate(
            flops=4 * tokens * width * kv, bytes_accessed=6 * tokens * width, transcendentals=0
        ),
        name="values_and_input_grad",
    )(x, w, cot, inv)


def body(
    layer_input,
    value_weight,
    norm_gain,
    cotangent,
    frag_global,
    frag_momentum,
    frag_snapshot,
    frag_local,
):
    x = layer_input[0]
    cot = cotangent[0]
    gain = norm_gain[0].astype(jnp.float32)[:, None]
    width = x.shape[1]
    rows, kv = value_weight[0].shape
    factor = float(width) ** (-0.5)

    own = (value_weight[0].astype(jnp.float32) * gain).astype(jnp.bfloat16)
    slab = lax.all_gather(own, "fsdp", axis=0, tiled=True, axis_index_groups=ZY_GROUPS)
    weight = lax.all_gather(slab, "fsdp", axis=0, axis_index_groups=X_GROUPS)
    weight = weight.reshape(NX, NZ, NY * rows, kv)

    partial, inv = weight_grad_partial(x, cot)
    summed = lax.psum_scatter(
        partial.reshape(NY * BLOCKS * rows, kv),
        "fsdp",
        scatter_dimension=0,
        tiled=True,
        axis_index_groups=Y_GROUPS,
    )
    pieces = lax.all_to_all(
        summed.reshape(BLOCKS, rows, kv), "fsdp", 0, 0, axis_index_groups=ZX_GROUPS
    )
    weight_grad = jnp.sum(pieces.astype(jnp.float32), axis=0) * (factor * gain)

    values, input_grad = values_and_input_grad(x, weight, cot, inv)

    mine = frag_snapshot[0]
    far = lax.ppermute(mine, "rep", OTHER_Z)
    near = lax.ppermute(mine, "rep", OTHER_CORE)
    far_near = lax.ppermute(far, "rep", OTHER_CORE)
    total = (mine.astype(jnp.float32) + near.astype(jnp.float32)) + (
        far.astype(jnp.float32) + far_near.astype(jnp.float32)
    )
    mean_delta = frag_global - total * (1.0 / lax.axis_size("rep"))
    new_momentum = outer_beta * frag_momentum + mean_delta
    new_global = frag_global - outer_rate * (mean_delta + outer_beta * new_momentum)
    new_local = (
        merge_weight * frag_local[0].astype(jnp.float32) + (1.0 - merge_weight) * new_global
    ).astype(jnp.bfloat16)
    return (
        values[None],
        input_grad[None],
        weight_grad[None],
        new_global,
        new_momentum,
        new_local[None],
    )


def solution(mesh):
    return jax.shard_map(
        body,
        mesh=mesh,
        in_specs=(
            P("rep", "fsdp", None),
            P("rep", "fsdp", None),
            P("rep", "fsdp"),
            P("rep", "fsdp", None),
            P("fsdp", None),
            P("fsdp", None),
            P("rep", "fsdp", None),
            P("rep", "fsdp", None),
        ),
        out_specs=(
            P("rep", "fsdp", None),
            P("rep", "fsdp", None),
            P("rep", "fsdp", None),
            P("fsdp", None),
            P("fsdp", None),
            P("rep", "fsdp", None),
        ),
        check_vma=False,
    )
```

time: 398 us -> 224 us (0.56)
  waiting for transfers between devices: 239 us -> 151 us
  blocking collectives: 82.4 us -> 0 us
  matrix products: 38.5 us -> 0 us
  Pallas kernels: 0 us -> 28.4 us
  other arithmetic: 21.5 us -> 7.65 us
  local copies, waits for them, and re-layouts: 1.65 us -> 11.2 us
  starting transfers between devices: 0.12 us -> 8.73 us
    reduce_scatter x1, waiting for transfers between devices: 172 us -> 29.3 us  [body(): lax.psum_scatter(partial.reshape(NY * BLOCKS * rows, kv), 'fsdp', scatter...]
    all_gather x1 -> x0, blocking collectives: 82.4 us -> none  [body(): gain_piece = lax.all_gather(gain_rows, 'fsdp', axis=0, tiled=True)]
    all_gather x1 -> x2, waiting for transfers between devices: 65.6 us -> 119 us  [the longest x1 62.4 us: body(): weight = lax.all_gather(slab, 'fsdp', axis=0, axis_index_groups=X_GROUPS)]
    dot_general x3 -> x0, matrix products: 38.5 us -> none  [the longest x1 13.9 us: body(): lax.dot_general(window, upstream, (((0,), (0,)), ((), ())), preferred_ele...]
    pallas_call x0 -> x2, Pallas kernels: none -> 28.4 us  [the longest x1 18.7 us: values_and_input_grad(): pl.pallas_call(functools.partial(input_grad_kernel, width, factor), grid=...]
    broadcast_in_dim x1 -> x0, other arithmetic: 10.6 us -> none  [body(): input_grad[None]]
    unnamed x14 -> x12, local copies, waits for them, and re-layouts: 1.65 us -> 11.2 us
    all_to_all x0 -> x1, starting transfers between devices: none -> 5.09 us  [body(): lax.all_to_all(summed.reshape(BLOCKS, rows, kv), 'fsdp', 0, 0, axis_index...]
  transfers between devices with their start and end apart: 3 -> 7, of which waited for: 2 -> 5; matrix products, arithmetic and copies ran while one was open for 14% -> 2% of each run, Pallas kernels for 0% -> 13%
where the time goes in v1:
time: 224 us; the launch traced here: 223 us
  waiting for transfers between devices  151 us (67%)
  Pallas kernels  28.4 us (13%)
  between operations  15.5 us (7%)
  local copies, waits for them, and re-layouts  11.2 us (5%)
  starting transfers between devices  8.73 us (4%)
  other arithmetic  7.65 us (3%)
    all_gather x1, waiting for transfers between devices, body(): weight = lax.all_gather(slab, 'fsdp', axis=0, axis_index_groups=X_GROUPS)  62.4 us
    all_gather x1, waiting for transfers between devices, body(): lax.all_gather(own, 'fsdp', axis=0, tiled=True, axis_index_groups=ZY_GROUPS)  57 us
    reduce_scatter x1, waiting for transfers between devices, body(): lax.psum_scatter(partial.reshape(NY * BLOCKS * rows, kv), 'fsdp', scatter...  29.3 us
    pallas_call x1, Pallas kernels, values_and_input_grad(): pl.pallas_call(functools.partial(input_grad_kernel, width, factor), grid=...  18.7 us
    unnamed x12, local copies, waits for them, and re-layouts  11.2 us
    pallas_call x1, Pallas kernels, weight_grad_partial(): pl.pallas_call(functools.partial(weight_grad_kernel, width), grid=(2, BLO...  9.77 us
    all_to_all x1, starting transfers between devices, body(): lax.all_to_all(summed.reshape(BLOCKS, rows, kv), 'fsdp', 0, 0, axis_index...  5.09 us
  transfers between devices with their start and end apart: 7, of which 5 were waited for; matrix products, arithmetic and copies ran while one was open for 2% of the time, Pallas kernels for 13%

profile of v1, /device:TPU:0, one launch (start us, length us, event | category | flops | bytes accessed | tf_op | source)
XLA Modules:
  0.0 222.5 jit_solution(13114679103379666583)
XLA Ops:
  8.0 0.0 all-gather.4.cloned.1.call-start
  8.0 0.7 convert_element_type.60
  8.7 1.8 fusion.3
  10.5 0.0 all-gather.4.cloned.1.call-update
  10.5 0.0 reduce-scatter.2.cloned.1.call-start
  10.6 0.0 copy-start.1
  10.6 3.4 %copy-done.1 = bf16[1,512,8192]{2,1,0:T(8,128)(2,1)S(1)} copy-done((bf16[1,512,8192]{2,1,0:T(8,128)(2,1)S(1)}, bf16[1,512,8192]{2,1,0:T(8,128)(2,1)}, u32[]{:S(2)}) %copy-start.1) | copy-done | bytes 8388632
  13.9 0.0 copy-start.3
  13.9 1.0 copy-done.3
  15.0 9.8 %weight_grad_partial.1 = (bf16[4,8,256,512]{3,2,1,0:T(8,128)(2,1)S(1)}, f32[512,128]{1,0:T(8,128)S(1)}) custom-call(bf16[512,8192]{1,0:T(8,128)(2,1)S(1)} %bitcast.24, bf16[512,512]{1,0:T(8,128)(2,1)S(1)} %bitcast.26), custom_call_target="tpu_custom_call" | custom-call | flops 4294967296 | bytes 16777216 | tf_op jit(solution)/shard_map/weight_grad_partial/pallas_call | solution.py:78
  24.8 0.0 copy-start
  24.8 3.4 %copy-done = bf16[4,8,256,512]{3,2,1,0:T(8,128)(2,1)} copy-done((bf16[4,8,256,512]{3,2,1,0:T(8,128)(2,1)}, bf16[4,8,256,512]{3,2,1,0:T(8,128)(2,1)S(1)}, u32[]{:S(2)}) %copy-start) | copy-done | bytes 8388632
  28.2 0.0 reduce-scatter.2.cloned.1.call-update
  28.2 0.0 copy-start.5
  28.2 0.0 all-gather.6.cloned.1.call-start
  28.3 57.0 %all-gather.4.cloned.1.call-done = bf16[2048,512]{1,0:T(8,128)(2,1)} async-done(((bf16[256,512]{1,0:T(8,128)(2,1)}), bf16[2048,512]{1,0:T(8,128)(2,1)}) %all-gather.4.cloned.1.call-update) | async-done | bytes 2097168 | tf_op jit(solution)/shard_map/all_gather | solution.py:200
  85.2 0.0 all-gather.6.cloned.1.call-update
  85.2 2.9 %collective-permute-start.1 = (bf16[256,1024]{1,0:T(8,128)(2,1)}, bf16[256,1024]{1,0:T(8,128)(2,1)}, u32[]{:S(2)}, u32[]{:S(2)}) collective-permute-start(bf16[256,1024]{1,0:T(8,128)(2,1)} %bitcast.10), channel_id=1, source_target_pairs={{0,64},{64,0},{32,96},{96,32},{1,65},{65,1},{33,97},{97,33},{2,66}... | collective-permute-start | bytes 1572872 | tf_op jit(solution)/shard_map/ppermute | solution.py:220
  88.2 29.3 %reduce-scatter.2.cloned.1.call-done = bf16[2048,512]{1,0:T(8,128)(2,1)} async-done(((bf16[8192,512]{1,0:T(8,128)(2,1)}), bf16[2048,512]{1,0:T(8,128)(2,1)}) %reduce-scatter.2.cloned.1.call-update) | async-done | bytes 2097168 | tf_op jit(solution)/shard_map/reduce_scatter | solution.py:205
  117.4 5.1 %all-to-all-start = ((bf16[8,256,512]{2,1,0:T(8,128)(2,1)}), bf16[8,256,512]{2,1,0:T(8,128)(2,1)S(1)}, u32[]{:S(2)}, u32[]{:S(2)}) async-start(bf16[8,256,512]{2,1,0:T(8,128)(2,1)} %bitcast.28), calls=%async_computation.1 | async-start | bytes 4194304 | tf_op jit(solution)/shard_map/all_to_all | solution.py:212
  122.5 0.0 copy-start.4
  122.5 0.1 collective-permute-start
  122.6 0.0 collective-permute-done.1
  122.6 0.5 collective-permute-start.2
  123.1 1.6 collective-permute-done
  124.7 0.7 collective-permute-done.2
  125.5 0.0 copy-done.5
  125.5 4.0 %fusion.2 = (bf16[1,256,1024]{2,1,0:T(8,128)(2,1)}, f32[256,1024]{1,0:T(8,128)}, f32[256,1024]{1,0:T(8,128)}) fusion(bf16[1,256,1024]{2,1,0:T(8,128)(2,1)S(1)} %copy-done.5, f32[256,1024]{1,0:T(8,128)} %param.12, bf16[256,1024]{1,0:T(8,128)(2,1)S(1)} %collective-permute-done.2, bf16[256,1024]{1,0:T(8,128)(2,1)} %collective-permute-done.1, ...), kind=kLoop, calls=%fused_computation.7 | loop fusion | flops 4980736 | bytes 7340032 | tf_op jit(solution)/shard_map/broadcast_in_dim | solution.py:238
  129.5 62.4 %all-gather.6.cloned.1.call-done = bf16[8192,512]{1,0:T(8,128)(2,1)} async-done(((bf16[2048,512]{1,0:T(8,128)(2,1)}), bf16[8192,512]{1,0:T(8,128)(2,1)}) %all-gather.6.cloned.1.call-update) | async-done | bytes 8388624 | tf_op jit(solution)/shard_map/all_gather | solution.py:201
  191.9 0.0 copy-done.4
  191.9 0.0 copy-start.2
  191.9 3.4 %copy-done.2 = bf16[1,512,8192]{2,1,0:T(8,128)(2,1)S(1)} copy-done((bf16[1,512,8192]{2,1,0:T(8,128)(2,1)S(1)}, bf16[1,512,8192]{2,1,0:T(8,128)(2,1)}, u32[]{:S(2)}) %copy-start.2) | copy-done | bytes 8388632
  195.3 18.7 %values_and_input_grad.1 = (bf16[512,512]{1,0:T(8,128)(2,1)}, bf16[512,8192]{1,0:T(8,128)(2,1)}) custom-call(bf16[512,8192]{1,0:T(8,128)(2,1)S(1)} %bitcast.25, bf16[4,2,1024,512]{3,2,1,0:T(8,128)(2,1)} %bitcast.31, bf16[512,512]{1,0:T(8,128)(2,1)S(1)} %bitcast.27, f32[512,128]{1,0:T(8,128)S(1)} %get-tuple-element.10.inv_ref), custom_call_target="tpu_custom_call" | custom-call | flops 8589934592 | bytes 25165824 | tf_op jit(solution)/shard_map/values_and_input_grad/pallas_call | solution.py:148
  213.9 0.0 all-to-all-done
  213.9 0.3 convert_reduce_fusion
  214.2 0.9 bitcast_multiply_fusion
  (1 shorter events, 0.0 us)
Async XLA Ops:
  8.0 77.2 %all-gather.4.cloned.1.call-start = ((), (), s32[]{:S(2)}) async-start(), calls=%async_computation.2 | async-start | bytes 2359296 | tf_op jit(solution)/shard_map/all_gather | solution.py:200
  10.5 106.9 %reduce-scatter.2.cloned.1.call-start = ((), (), s32[]{:S(2)}) async-start(), calls=%async_computation.3 | async-start | bytes 10485760 | tf_op jit(solution)/shard_map/reduce_scatter | solution.py:205
  10.6 3.4 %copy-start.1 = (bf16[1,512,8192]{2,1,0:T(8,128)(2,1)S(1)}, bf16[1,512,8192]{2,1,0:T(8,128)(2,1)}, u32[]{:S(2)}) copy-start(bf16[1,512,8192]{2,1,0:T(8,128)(2,1)} %param.8) | copy-start | bytes 25165828
  13.9 1.0 copy-start.3
  24.8 3.4 %copy-start = (bf16[4,8,256,512]{3,2,1,0:T(8,128)(2,1)}, bf16[4,8,256,512]{3,2,1,0:T(8,128)(2,1)S(1)}, u32[]{:S(2)}) copy-start(bf16[4,8,256,512]{3,2,1,0:T(8,128)(2,1)S(1)} %get-tuple-element.13) | copy-start | bytes 25165828
  28.2 97.3 %copy-start.5 = (bf16[1,256,1024]{2,1,0:T(8,128)(2,1)S(1)}, bf16[1,256,1024]{2,1,0:T(8,128)(2,1)}, u32[]{:S(2)}) copy-start(bf16[1,256,1024]{2,1,0:T(8,128)(2,1)} %param.15) | copy-start | bytes 1572868
  28.2 163.7 %all-gather.6.cloned.1.call-start = ((), (), s32[]{:S(2)}) async-start(), calls=%async_computation.4 | async-start | bytes 10485760 | tf_op jit(solution)/shard_map/all_gather | solution.py:201
  85.2 37.4 %collective-permute-start.1 = (bf16[256,1024]{1,0:T(8,128)(2,1)}, bf16[256,1024]{1,0:T(8,128)(2,1)}, u32[]{:S(2)}, u32[]{:S(2)}) collective-permute-start(bf16[256,1024]{1,0:T(8,128)(2,1)} %bitcast.10), channel_id=1, source_target_pairs={{0,64},{64,0},{32,96},{96,32},{1,65},{65,1},{33,97},{97,33},{2,66}... | collective-permute-start | bytes 1572872 | tf_op jit(solution)/shard_map/ppermute | solution.py:220
  117.4 96.5 %all-to-all-start = ((bf16[8,256,512]{2,1,0:T(8,128)(2,1)}), bf16[8,256,512]{2,1,0:T(8,128)(2,1)S(1)}, u32[]{:S(2)}, u32[]{:S(2)}) async-start(bf16[8,256,512]{2,1,0:T(8,128)(2,1)} %bitcast.28), calls=%async_computation.1 | async-start | bytes 4194304 | tf_op jit(solution)/shard_map/all_to_all | solution.py:212
  122.5 69.4 %copy-start.4 = (bf16[1,512,512]{2,1,0:T(8,128)(2,1)S(1)}, bf16[1,512,512]{2,1,0:T(8,128)(2,1)}, u32[]{:S(2)}) copy-start(bf16[1,512,512]{2,1,0:T(8,128)(2,1)} %param.11) | copy-start | bytes 1572868
  122.5 2.2 collective-permute-start
  122.6 2.8 %collective-permute-start.2 = (bf16[256,1024]{1,0:T(8,128)(2,1)}, bf16[256,1024]{1,0:T(8,128)(2,1)S(1)}, u32[]{:S(2)}, u32[]{:S(2)}) collective-permute-start(bf16[256,1024]{1,0:T(8,128)(2,1)} %collective-permute-done.1), channel_id=1, source_target_pairs={{0,32},{32,0},{64,96},{96,64},{1,33},{33,1},{65,97},{97,65},{2,34}... | collective-permute-start | bytes 1572872 | tf_op jit(solution)/shard_map/ppermute | solution.py:222
  191.9 3.4 %copy-start.2 = (bf16[1,512,8192]{2,1,0:T(8,128)(2,1)S(1)}, bf16[1,512,8192]{2,1,0:T(8,128)(2,1)}, u32[]{:S(2)}) copy-start(bf16[1,512,8192]{2,1,0:T(8,128)(2,1)} %param.8) | copy-start | bytes 25165828
Sparse Core Ops, SparseCore 0:
  11.0 74.1 all-gather.3
  86.9 104.9 all-gather.5
Sparse Core Ops, SparseCore 1:
  28.3 89.1 reduce-scatter.1

commit v2 on v0

v2 whole, which is shorter than its diff:
```python
import functools

import jax
import jax.numpy as jnp
from jax import lax
from jax.experimental import pallas as pl
from jax.experimental.pallas import tpu as pltpu
from jax.sharding import PartitionSpec as P

epsilon = 1e-05
outer_rate = 0.7
outer_beta = 0.9
merge_weight = 0.5

NZ, NX, NY = 2, 4, 4
BLOCKS = NZ * NX
MIB = 1 << 20
VMEM_LIMIT = 56 * MIB


def _index(z, x, y):
    return (z * NX + x) * NY + y


ZY_GROUPS = [[_index(z, x, y) for z in range(NZ) for y in range(NY)] for x in range(NX)]
X_GROUPS = [[_index(z, x, y) for x in range(NX)] for z in range(NZ) for y in range(NY)]


def _shift(dz, dx, dy):
    return [
        (_index(z, x, y), _index((z + dz) % NZ, (x + dx) % NX, (y + dy) % NY))
        for z in range(NZ)
        for x in range(NX)
        for y in range(NY)
    ]


Z_SWAP = _shift(1, 0, 0)
X_UP, X_DOWN = _shift(0, 1, 0), _shift(0, -1, 0)
Y_UP, Y_DOWN = _shift(0, 0, 1), _shift(0, 0, -1)
MIB = 1 << 20
VMEM_LIMIT = 56 * MIB


def _index(z, x, y):
    return (z * NX + x) * NY + y


ZY_GROUPS = [[_index(z, x, y) for z in range(NZ) for y in range(NY)] for x in range(NX)]
ZX_GROUPS = [[_index(z, x, y) for z in range(NZ) for x in range(NX)] for y in range(NY)]


def _shift(dz, dx, dy):
    return [
        (_index(z, x, y), _index((z + dz) % NZ, (x + dx) % NX, (y + dy) % NY))
        for z in range(NZ)
        for x in range(NX)
        for y in range(NY)
    ]


Z_SWAP = _shift(1, 0, 0)
X_UP, X_DOWN = _shift(0, 1, 0), _shift(0, -1, 0)
Y_UP, Y_DOWN = _shift(0, 0, 1), _shift(0, 0, -1)
OTHER_CORE = [(0, 1), (1, 0), (2, 3), (3, 2)]
OTHER_Z = [(0, 2), (2, 0), (1, 3), (3, 1)]


HBM = pl.BlockSpec(memory_space=pl.ANY)
VMEM = pl.BlockSpec(memory_space=pltpu.VMEM)
SMEM = pl.BlockSpec(memory_space=pltpu.SMEM)
CHUNKS = 8

FIRST = ((2, 0), (1, 1), (2, 1), (NX - 1, 0))
REST = ((1, 0), (NX - 1, 1), (0, 0), (0, 1))


def norm_kernel(width, x_ref, cot_ref, inv_ref, scaled_ref, held, sems):
    chunks, rows = held.shape[:2]

    def copy(k):
        return pltpu.make_async_copy(x_ref.at[pl.ds(k * rows, rows)], held.at[k], sems.at[k])

    for k in range(chunks):
        copy(k).start()
    for k in range(chunks):
        copy(k).wait()

        def add(c, total):
            wide = held[k, :, pl.ds(pl.multiple_of(c * 512, 512), 512)].astype(jnp.float32)
            squares = wide * wide
            return (
                total
                + (squares[:, :128] + squares[:, 128:256])
                + (squares[:, 256:384] + squares[:, 384:])
            )

        total = lax.fori_loop(0, width // 512, add, jnp.zeros((rows, 128), jnp.float32), unroll=4)
        inv = 1.0 / jnp.sqrt(jnp.sum(total, axis=1, keepdims=True) / width + epsilon)
        here = pl.ds(k * rows, rows)
        inv_ref[here, :] = jnp.broadcast_to(inv, (rows, 128))
        scaled_ref[here, :] = (cot_ref[here, :].astype(jnp.float32) * inv).astype(jnp.bfloat16)


def norm_and_scaled_cotangent(x, cot):
    tokens, width = x.shape
    kv = cot.shape[1]
    return pl.pallas_call(
        functools.partial(norm_kernel, width),
        in_specs=[HBM, VMEM],
        out_specs=[VMEM, VMEM],
        out_shape=[
            jax.ShapeDtypeStruct((tokens, 128), jnp.float32),
            jax.ShapeDtypeStruct((tokens, kv), jnp.bfloat16),
        ],
        scratch_shapes=[
            pltpu.VMEM((CHUNKS, tokens // CHUNKS, width), jnp.bfloat16),
            pltpu.SemaphoreType.DMA((CHUNKS,)),
        ],
        compiler_params=pltpu.CompilerParams(vmem_limit_bytes=VMEM_LIMIT),
        cost_estimate=pl.CostEstimate(
            flops=8 * tokens * width, bytes_accessed=2 * tokens * width, transcendentals=0
        ),
        name="norm_and_scaled_cotangent",
    )(x, cot)


def weight_grad_kernel(todo, place_ref, x_ref, scaled_ref, *rest):
    outs, (held, stage, load_sems, store_sems) = rest[:4], rest[4:]
    cols = held.shape[2]
    rows = cols // NY // 2
    x = place_ref[0]

    def load(k):
        d, z = todo[k]
        j = z * NX + lax.rem(x + d, NX)
        columns = pl.ds(pl.multiple_of(j * cols, cols), cols)
        return pltpu.make_async_copy(x_ref.at[:, columns], held.at[k], load_sems.at[k])

    def store(half, k):
        n = half * len(todo) + k
        where = outs[n // 2].at[pl.ds((n % 2) * NY * rows, NY * rows)]
        return pltpu.make_async_copy(stage.at[n], where, store_sems.at[n])

    for k in range(len(todo)):
        load(k).start()
    for k in range(len(todo)):
        load(k).wait()
        for half in (0, 1):
            for p in range(NY):
                stage[half * len(todo) + k, p * rows : (p + 1) * rows, :] = lax.dot_general(
                    held[k, :, (2 * p + half) * rows : (2 * p + half + 1) * rows],
                    scaled_ref[...],
                    (((0,), (0,)), ((), ())),
                    preferred_element_type=jnp.float32,
                ).astype(stage.dtype)
            store(half, k).start()
    for k in range(len(todo)):
        for half in (0, 1):
            store(half, k).wait()


def weight_grad_chunks(x, scaled, place, todo, dtype):
    tokens, width = x.shape
    kv = scaled.shape[1]
    cols = width // BLOCKS
    rows = cols // NY // 2
    return pl.pallas_call(
        functools.partial(weight_grad_kernel, todo),
        in_specs=[SMEM, HBM, VMEM],
        out_specs=[HBM] * 4,
        out_shape=[jax.ShapeDtypeStruct((2 * NY * rows, kv), dtype)] * 4,
        scratch_shapes=[
            pltpu.VMEM((len(todo), tokens, cols), jnp.bfloat16),
            pltpu.VMEM((2 * len(todo), NY * rows, kv), dtype),
            pltpu.SemaphoreType.DMA((len(todo),)),
            pltpu.SemaphoreType.DMA((2 * len(todo),)),
        ],
        compiler_params=pltpu.CompilerParams(vmem_limit_bytes=VMEM_LIMIT),
        cost_estimate=pl.CostEstimate(
            flops=tokens * width * kv, bytes_accessed=2 * tokens * width, transcendentals=0
        ),
        name="weight_grad_chunks",
    )(place, x, scaled)


def assemble_kernel(plan, rows_in, *refs):
    arrays, refs = refs[: len(rows_in)], refs[len(rows_in) :]
    outs, refs = refs[: len(plan)], refs[len(plan) :]
    stages, refs = refs[: len(plan)], refs[len(plan) :]
    *held, load_sems, store_sems = refs

    loads = []
    n = taken = 0
    for stage, segments in zip(stages, plan):
        start = 0
        for rows, sources in segments:
            here = []
            for array, first in sources:
                if len(sources) == 1:
                    target = stage.at[pl.ds(start, rows)]
                else:
                    target = held[taken]
                    taken += 1
                source = arrays[array].at[pl.ds(first, rows)]
                here.append((pltpu.make_async_copy(source, target, load_sems.at[n]), target))
                n += 1
            loads.append(here)
            start += rows
    for here in loads:
        for copy, _ in here:
            copy.start()
    stores = []
    k = 0
    for m, (out, stage, segments) in enumerate(zip(outs, stages, plan)):
        start = 0
        for rows, sources in segments:
            here = loads[k]
            k += 1
            for copy, _ in here:
                copy.wait()
            if len(sources) > 1:
                total = here[0][1][...].astype(jnp.float32)
                for _, target in here[1:]:
                    total = total + target[...].astype(jnp.float32)
                stage[start : start + rows, :] = total.astype(stage.dtype)
            start += rows
        stores.append(pltpu.make_async_copy(stage, out, store_sems.at[m]))
        stores[-1].start()
    for store in stores:
        store.wait()


def assemble(arrays, plan):
    kv = arrays[0].shape[1]
    sizes = [sum(rows for rows, _ in segments) for segments in plan]
    held = [
        pltpu.VMEM((rows, kv), arrays[array].dtype)
        for segments in plan
        for rows, sources in segments
        if len(sources) > 1
        for array, _ in sources
    ]
    copies = sum(len(sources) for segments in plan for _, sources in segments)
    return pl.pallas_call(
        functools.partial(assemble_kernel, plan, [a.shape[0] for a in arrays]),
        in_specs=[HBM] * len(arrays),
        out_specs=[HBM] * len(plan),
        out_shape=[jax.ShapeDtypeStruct((size, kv), jnp.bfloat16) for size in sizes],
        scratch_shapes=[pltpu.VMEM((size, kv), jnp.bfloat16) for size in sizes]
        + held
        + [pltpu.SemaphoreType.DMA((copies,)), pltpu.SemaphoreType.DMA((len(plan),))],
        compiler_params=pltpu.CompilerParams(vmem_limit_bytes=VMEM_LIMIT),
        cost_estimate=pl.CostEstimate(
            flops=sum(sizes) * kv, bytes_accessed=6 * sum(sizes) * kv, transcendentals=0
        ),
        name="assemble",
    )(*arrays)


def strip_copy(x_ref, strips, sems, owners_ref, k):
    rows = strips.shape[2]
    columns = pl.ds(pl.multiple_of(owners_ref[k] * rows, rows), rows)
    return pltpu.make_async_copy(x_ref.at[:, columns], strips.at[k], sems.at[k])


def projection_kernel(count, owners_ref, x_ref, *rest):
    *refs, total_ref, strips, held_w, w_sems, x_sems = rest
    rows = strips.shape[2]
    per_array = count // len(refs)

    def weight(k):
        block = refs[k // per_array].at[pl.ds((k % per_array) * rows, rows)]
        return pltpu.make_async_copy(block, held_w.at[k], w_sems.at[k])

    for k in range(count):
        strip_copy(x_ref, strips, x_sems, owners_ref, k).start()
        weight(k).start()
    for k in range(count):
        strip_copy(x_ref, strips, x_sems, owners_ref, k).wait()
        weight(k).wait()
        part = jnp.dot(strips[k], held_w[k], preferred_element_type=jnp.float32)
        total_ref[...] = part if k == 0 else total_ref[...] + part


def projection(x, arrays, owners):
    tokens, width = x.shape
    kv = arrays[0].shape[1]
    rows = width // BLOCKS // NY
    count = NX * len(arrays)
    return pl.pallas_call(
        functools.partial(projection_kernel, count),
        in_specs=[SMEM, HBM] + [HBM] * len(arrays),
        out_specs=VMEM,
        out_shape=jax.ShapeDtypeStruct((tokens, kv), jnp.float32),
        scratch_shapes=[
            pltpu.VMEM((count, tokens, rows), jnp.bfloat16),
            pltpu.VMEM((count, rows, kv), jnp.bfloat16),
            pltpu.SemaphoreType.DMA((count,)),
            pltpu.SemaphoreType.DMA((count,)),
        ],
        compiler_params=pltpu.CompilerParams(vmem_limit_bytes=VMEM_LIMIT),
        cost_estimate=pl.CostEstimate(
            flops=2 * tokens * rows * count * kv,
            bytes_accessed=4 * tokens * rows * count,
            transcendentals=0,
        ),
        name="projection",
    )(owners, x, *arrays)


def input_grad_kernel(width, factor, late, owners_ref, x_ref, cot_ref, inv_ref, total_ref, *rest):
    *refs, val_ref, out_ref, held_x, held_w, strips, stage, w_sems, x_sems, strip_sems, out_sems = rest
    tokens, cols = held_x.shape[1:]
    rows, kv = held_w.shape[1:]
    first = BLOCKS * NY - late
    per_side = len(refs) // NZ

    def weight(side, n, k):
        array = side * per_side + n
        y = lax.rem(owners_ref[array * NX], NY)
        where = held_w.at[(side * NX + k) * NY + y]
        return pltpu.make_async_copy(
            refs[array].at[pl.ds(k * rows, rows)], where, w_sems.at[array * NX + k]
        )

    def columns(ref, held, sems, side, k, out):
        j = owners_ref[side * per_side * NX + k] // NY
        where = ref.at[:, pl.ds(pl.multiple_of(j * cols, cols), cols)]
        step = side * NX + k
        if out:
            return pltpu.make_async_copy(held.at[step], where, sems.at[step])
        return pltpu.make_async_copy(where, held.at[step], sems.at[step])

    def strip(side, k):
        n = side * NX + k
        owner = owners_ref[(side * per_side + per_side - 1) * NX + k]
        where = x_ref.at[:, pl.ds(pl.multiple_of(owner * rows, rows), rows)]
        return pltpu.make_async_copy(where, strips.at[n], strip_sems.at[n])

    steps = [(side, k) for side in range(NZ) for k in range(NX)]
    for side, k in steps:
        strip(side, k).start()
        weight(side, per_side - 1, k).start()
    for side, k in steps:
        for n in range(per_side - 1):
            weight(side, n, k).start()
        columns(x_ref, held_x, x_sems, side, k, False).start()
    total = total_ref[...]
    for side, k in steps:
        strip(side, k).wait()
        weight(side, per_side - 1, k).wait()
        y = lax.rem(owners_ref[(side * per_side + per_side - 1) * NX], NY)
        total = total + jnp.dot(
            strips[side * NX + k],
            held_w[(side * NX + k) * NY + y],
            preferred_element_type=jnp.float32,
        )
    inv = inv_ref[:, :1]
    values = total * (factor * inv)
    val_ref[...] = values.astype(jnp.bfloat16)
    mean = jnp.sum(cot_ref[...].astype(jnp.float32) * values, axis=1, keepdims=True) / width
    shift = mean * inv * inv
    scale = factor * inv

    for side, k in steps:
        for n in range(per_side - 1):
            weight(side, n, k).wait()
        columns(x_ref, held_x, x_sems, side, k, False).wait()
        step = side * NX + k
        for n in range(NY):
            adjoint = lax.dot_general(
                cot_ref[...],
                held_w[step * NY + n],
                (((1,), (1,)), ((), ())),
                preferred_element_type=jnp.float32,
            )
            here = slice(n * rows, (n + 1) * rows)
            stage[step, :, here] = (
                adjoint * scale - held_x[step, :, here].astype(jnp.float32) * shift
            ).astype(jnp.bfloat16)
        columns(out_ref, stage, out_sems, side, k, True).start()
    for side, k in steps:
        columns(out_ref, stage, out_sems, side, k, True).wait()


def values_and_input_grad(x, arrays, owners, total, cot, inv):
    late = NZ * NX
    tokens, width = x.shape
    kv = cot.shape[1]
    cols = width // BLOCKS
    rows = cols // NY
    factor = float(width) ** (-0.5)
    return pl.pallas_call(
        functools.partial(input_grad_kernel, width, factor, late),
        in_specs=[SMEM, HBM, VMEM, VMEM, VMEM] + [HBM] * len(arrays),
        out_specs=[VMEM, HBM],
        out_shape=[
            jax.ShapeDtypeStruct((tokens, kv), jnp.bfloat16),
            jax.ShapeDtypeStruct((tokens, width), jnp.bfloat16),
        ],
        scratch_shapes=[
            pltpu.VMEM((BLOCKS, tokens, cols), jnp.bfloat16),
            pltpu.VMEM((BLOCKS * NY, rows, kv), jnp.bfloat16),
            pltpu.VMEM((late, tokens, rows), jnp.bfloat16),
            pltpu.VMEM((BLOCKS, tokens, cols), jnp.bfloat16),
            pltpu.SemaphoreType.DMA((BLOCKS * NY,)),
            pltpu.SemaphoreType.DMA((BLOCKS,)),
            pltpu.SemaphoreType.DMA((late,)),
            pltpu.SemaphoreType.DMA((BLOCKS,)),
        ],
        compiler_params=pltpu.CompilerParams(vmem_limit_bytes=VMEM_LIMIT),
        cost_estimate=pl.CostEstimate(
            flops=2 * tokens * width * kv, bytes_accessed=6 * tokens * width, transcendentals=0
        ),
        name="values_and_input_grad",
    )(owners, x, cot, inv, total, *arrays)


def send(block, where):
    return lax.ppermute(block, "fsdp", where)


def block_order(z, y):
    places = [(dz, dy) for dz in (0, 1) for dy in (0, -1, 1)] + [(0, 2), (1, 2)]
    return jnp.stack(
        [_index((z + dz) % NZ, k, (y + dy) % NY) for dz, dy in places for k in range(NX)]
    ).astype(jnp.int32)


def final_order(owners):
    near, others, far = owners[: 3 * NX], owners[3 * NX : 6 * NX], owners[6 * NX :]
    return jnp.concatenate([near, far[:NX], others, far[NX:]])


def body(
    layer_input,
    value_weight,
    norm_gain,
    cotangent,
    frag_global,
    frag_momentum,
    frag_snapshot,
    frag_local,
):
    x = layer_input[0]
    cot = cotangent[0]
    gain = norm_gain[0].astype(jnp.float32)[:, None]
    width = x.shape[1]
    rows, kv = value_weight[0].shape
    half = rows // 2
    factor = float(width) ** (-0.5)
    me = lax.axis_index("fsdp")
    place = jnp.reshape((me // NY) % NX, (1,)).astype(jnp.int32)
    f32 = jnp.float32

    def after(values, *others):
        return lax.optimization_barrier((values, others))[0]

    own = (value_weight[0].astype(f32) * gain).astype(jnp.bfloat16)
    slab = lax.all_to_all(
        jnp.broadcast_to(own, (NX, rows, kv)), "fsdp", 0, 0, axis_index_groups=X_GROUPS
    ).reshape(NX * rows, kv)
    inv, scaled = norm_and_scaled_cotangent(x, cot)

    chunk = NY * half
    sent = weight_grad_chunks(x, scaled, place, FIRST, jnp.bfloat16)
    got = [[send(sent[0], X_UP), send(sent[1], X_DOWN)]]
    below, above, other = send(slab, Y_UP), send(slab, Y_DOWN), send(slab, Z_SWAP)

    first = (got[0], below, above, other)
    messages = after(sent[2:], got[0])
    got.append([send(m, r) for m, r in zip(messages, (X_UP, X_DOWN))])
    message = after(other, below, above)
    other_below, other_above = send(message, Y_UP), send(message, Y_DOWN)

    owners = block_order(me // (NX * NY), me % NY)
    near, others = [slab, below, above], [other, other_below, other_above]
    kept = weight_grad_chunks(x, scaled, place, REST, f32)
    add = [[(chunk, [(0, way * chunk), (1 + way, 0)])] for way in (0, 1)]
    messages = after(assemble([kept[0], *got[0]], add), got[1])
    then = [[send(m, r) for m, r in zip(messages, (X_UP, X_DOWN))]]
    messages = after([below, other_above], other_below)
    far = [send(messages[0], Y_UP), send(messages[1], Y_DOWN)]
    messages = after(assemble([kept[2], *got[1]], add), then[0])
    then.append([send(m, r) for m, r in zip(messages, (X_UP, X_DOWN))])

    mine = after(frag_snapshot[0], *first)
    everyone = jnp.broadcast_to(mine, (lax.axis_size("rep"), *mine.shape))
    total = jnp.sum(lax.all_to_all(everyone, "rep", 0, 0).astype(f32), axis=0)
    mean_delta = frag_global - total * (1.0 / lax.axis_size("rep"))
    new_momentum = outer_beta * frag_momentum + mean_delta
    new_global = frag_global - outer_rate * (mean_delta + outer_beta * new_momentum)
    new_local = (
        merge_weight * frag_local[0].astype(f32) + (1.0 - merge_weight) * new_global
    ).astype(jnp.bfloat16)

    product = projection(x, [*near, *others], owners)

    arrays = [kept[1], *got[0], *then[0], kept[3], *got[1], *then[1]]
    segments = []
    for k in range(BLOCKS):
        z, start = k // NY, k % NY * half
        for n in (0, 5):
            came = [(n + 2 - z, chunk + start), (n + 3 + z, start)]
            segments.append((half, [(n, k * half), *came]))
    (ring,) = assemble(after(arrays, far, product, new_local), [segments])
    group = lax.all_to_all(ring.reshape(BLOCKS, rows, kv), "fsdp", 0, 0, axis_index_groups=ZY_GROUPS)

    values, input_grad = values_and_input_grad(
        x, [*near, far[0], *others, far[1]], final_order(owners), product, cot, inv
    )
    group = after(group, input_grad)
    weight_grad = jnp.sum(group.astype(f32), axis=0) * (factor * gain)
    return (
        values[None],
        input_grad[None],
        weight_grad[None],
        new_global,
        new_momentum,
        new_local[None],
    )


def solution(mesh):
    return jax.shard_map(
        body,
        mesh=mesh,
        in_specs=(
            P("rep", "fsdp", None),
            P("rep", "fsdp", None),
            P("rep", "fsdp"),
            P("rep", "fsdp", None),
            P("fsdp", None),
            P("fsdp", None),
            P("rep", "fsdp", None),
            P("rep", "fsdp", None),
        ),
        out_specs=(
            P("rep", "fsdp", None),
            P("rep", "fsdp", None),
            P("rep", "fsdp", None),
            P("fsdp", None),
            P("fsdp", None),
            P("rep", "fsdp", None),
        ),
        check_vma=False,
    )
```

time: 398 us -> 151 us (0.38)
  waiting for transfers between devices: 239 us -> 44.4 us
  blocking collectives: 82.4 us -> 0 us
  Pallas kernels: 0 us -> 52.9 us
  starting transfers between devices: 0.12 us -> 38.8 us
  matrix products: 38.5 us -> 0 us
  other arithmetic: 21.5 us -> 5.2 us
  between operations: 15.5 us -> 0.83 us
  local copies, waits for them, and re-layouts: 1.65 us -> 7.3 us
    reduce_scatter x1 -> x0, waiting for transfers between devices: 172 us -> none  [body(): lax.psum_scatter(factor * lax.dot_general(window, upstream, (((0,), (0,))...]
    all_gather x1 -> x0, blocking collectives: 82.4 us -> none  [body(): gain_piece = lax.all_gather(gain_rows, 'fsdp', axis=0, tiled=True)]
    all_gather x1 -> x0, waiting for transfers between devices: 65.6 us -> none  [body(): weight_piece = lax.all_gather(weight_rows, 'fsdp', axis=0, tiled=True)]
    pallas_call x0 -> x8, Pallas kernels: none -> 52.9 us  [the longest x1 16.2 us: values_and_input_grad(): pl.pallas_call(functools.partial(input_grad_kernel, width, factor, late),...]
    dot_general x3 -> x0, matrix products: 38.5 us -> none  [the longest x1 13.9 us: body(): lax.dot_general(window, upstream, (((0,), (0,)), ((), ())), preferred_ele...]
    ppermute x0 -> x15, waiting for transfers between devices: none -> 35.6 us  [send(): return lax.ppermute(block, 'fsdp', where)]
    ppermute x0 -> x15, starting transfers between devices: none -> 24.4 us  [send(): return lax.ppermute(block, 'fsdp', where)]
    all_to_all x0 -> x3, starting transfers between devices: none -> 14.4 us  [the longest x1 5.16 us: body(): total = jnp.sum(lax.all_to_all(everyone, 'rep', 0, 0).astype(f32), axis=0)]
  transfers between devices with their start and end apart: 3 -> 18, of which waited for: 2 -> 9; matrix products, arithmetic and copies ran while one was open for 14% -> 4% of each run, Pallas kernels for 0% -> 32%
where the time goes in v2:
time: 151 us; the launch traced here: 150 us
  Pallas kernels  52.9 us (35%)
  waiting for transfers between devices  44.4 us (29%)
  starting transfers between devices  38.8 us (26%)
  local copies, waits for them, and re-layouts  7.3 us (5%)
  other arithmetic  5.2 us (3%)
    ppermute x15, waiting for transfers between devices, send(): return lax.ppermute(block, 'fsdp', where)  35.6 us
    ppermute x15, starting transfers between devices, send(): return lax.ppermute(block, 'fsdp', where)  24.4 us
    pallas_call x1, Pallas kernels, values_and_input_grad(): pl.pallas_call(functools.partial(input_grad_kernel, width, factor, late),...  16.2 us
    pallas_call x2, Pallas kernels, weight_grad_chunks(): pl.pallas_call(functools.partial(weight_grad_kernel, todo), in_specs=[SME...  12.6 us
    pallas_call x3, Pallas kernels, assemble(): pl.pallas_call(functools.partial(assemble_kernel, plan, [a.shape[0] for a...  10.8 us
    all_to_all x1, waiting for transfers between devices, body(): lax.all_to_all(ring.reshape(BLOCKS, rows, kv), 'fsdp', 0, 0, axis_index_g...  8.84 us
    pallas_call x1, Pallas kernels, projection(): pl.pallas_call(functools.partial(projection_kernel, count), in_specs=[SME...  7.5 us
    pallas_call x1, Pallas kernels, norm_and_scaled_cotangent(): pl.pallas_call(functools.partial(norm_kernel, width), in_specs=[HBM, VMEM...  5.73 us
  transfers between devices with their start and end apart: 18, of which 9 were waited for; matrix products, arithmetic and copies ran while one was open for 4% of the time, Pallas kernels for 32%

profile of v2, /device:TPU:0, one launch (start us, length us, event | category | flops | bytes accessed | tf_op | source)
XLA Modules:
  0.0 149.5 jit_solution(7545826526815240555)
XLA Ops:
  0.6 0.7 convert_element_type.48
  1.3 1.1 fusion.2
  2.4 1.1 broadcast_in_dim.17
  3.4 4.4 %all-to-all-start = ((bf16[4,256,512]{2,1,0:T(8,128)(2,1)}), bf16[4,256,512]{2,1,0:T(8,128)(2,1)S(1)}, u32[]{:S(2)}, u32[]{:S(2)}) async-start(bf16[4,256,512]{2,1,0:T(8,128)(2,1)} %broadcast_in_dim.17), calls=%async_computation | async-start | bytes 2097152 | tf_op jit(solution)/shard_map/all_to_all | solution.py:461
  7.8 5.7 %norm_and_scaled_cotangent.1 = (f32[512,128]{1,0:T(8,128)}, bf16[512,512]{1,0:T(8,128)(2,1)}) custom-call(bf16[512,8192]{1,0:T(8,128)(2,1)} %bitcast.50, bf16[512,512]{1,0:T(8,128)(2,1)} %bitcast.61), custom_call_target="tpu_custom_call" | custom-call | flops 33554432 | bytes 8388608 | tf_op jit(solution)/shard_map/norm_and_scaled_cotangent/pallas_call | solution.py:108
  13.5 6.2 %weight_grad_chunks.3 = (bf16[1024,512]{1,0:T(8,128)(2,1)}, bf16[1024,512]{1,0:T(8,128)(2,1)}, bf16[1024,512]{1,0:T(8,128)(2,1)}, bf16[1024,512]{1,0:T(8,128)(2,1)}) custom-call(s32[1]{0:T(128)} %bitcast.39.place_ref, bf16[512,8192]{1,0:T(8,128)(2,1)} %bitcast.51, bf16[512,512]{1,0:T(8,128)(2,1)} %get-tuple-element.49.scaled_ref), custom_call_target="tpu_custom_call" | custom-call | flops 2147483648 | bytes 8388608 | tf_op jit(solution)/shard_map/weight_grad_chunks/pallas_call | solution.py:168
  19.7 2.1 %collective-permute-start.7 = (bf16[1024,512]{1,0:T(8,128)(2,1)}, bf16[1024,512]{1,0:T(8,128)(2,1)S(1)}, u32[]{:S(2)}, u32[]{:S(2)}) collective-permute-start(bf16[1024,512]{1,0:T(8,128)(2,1)} %get-tuple-element.51), channel_id=1, source_target_pairs={{0,4},{1,5},{2,6},{3,7},{4,8},{5,9},{6,10},{7,11},{8,12},{9,13},{1... | collective-permute-start | bytes 3145736 | tf_op jit(solution)/shard_map/ppermute | solution.py:421
  21.8 1.3 collective-permute-start.8
  23.1 1.6 %collective-permute-start = (bf16[1024,512]{1,0:T(8,128)(2,1)S(1)}, bf16[1024,512]{1,0:T(8,128)(2,1)S(1)}, u32[]{:S(2)}, u32[]{:S(2)}) collective-permute-start(bf16[1024,512]{1,0:T(8,128)(2,1)S(1)} %bitcast.55), channel_id=1, source_target_pairs={{0,1},{1,2},{2,3},{3,0},{4,5},{5,6},{6,7},{7,4},{8,9},{9,10},{10,1... | collective-permute-start | bytes 3145736 | tf_op jit(solution)/shard_map/ppermute | solution.py:421
  24.7 1.7 %collective-permute-start.1 = (bf16[1024,512]{1,0:T(8,128)(2,1)S(1)}, bf16[1024,512]{1,0:T(8,128)(2,1)S(1)}, u32[]{:S(2)}, u32[]{:S(2)}) collective-permute-start(bf16[1024,512]{1,0:T(8,128)(2,1)S(1)} %bitcast.56), channel_id=1, source_target_pairs={{0,3},{1,0},{2,1},{3,2},{4,7},{5,4},{6,5},{7,6},{8,11},{9,8},{10,9... | collective-permute-start | bytes 3145736 | tf_op jit(solution)/shard_map/ppermute | solution.py:421
  26.4 1.9 %collective-permute-start.2 = (bf16[1024,512]{1,0:T(8,128)(2,1)S(1)}, bf16[1024,512]{1,0:T(8,128)(2,1)S(1)}, u32[]{:S(2)}, u32[]{:S(2)}) collective-permute-start(bf16[1024,512]{1,0:T(8,128)(2,1)S(1)} %bitcast.57), channel_id=1, source_target_pairs={{0,16},{1,17},{2,18},{3,19},{4,20},{5,21},{6,22},{7,23},{8,24},{9,... | collective-permute-start | bytes 3145736 | tf_op jit(solution)/shard_map/ppermute | solution.py:421
  28.3 17.6 %collective-permute-done.7.refs_1_ = bf16[1024,512]{1,0:T(8,128)(2,1)S(1)} collective-permute-done((bf16[1024,512]{1,0:T(8,128)(2,1)}, bf16[1024,512]{1,0:T(8,128)(2,1)S(1)}, u32[]{:S(2)}, u32[]{:S(2)}) %collective-permute-start.7) | collective-permute-done | bytes 1048608 | tf_op jit(solution)/shard_map/ppermute | solution.py:421
  45.9 0.2 collective-permute-done.8.refs_2_
  46.1 2.8 %collective-permute-start.10 = (bf16[1024,512]{1,0:T(8,128)(2,1)}, bf16[1024,512]{1,0:T(8,128)(2,1)}, u32[]{:S(2)}, u32[]{:S(2)}) collective-permute-start(bf16[1024,512]{1,0:T(8,128)(2,1)} %get-tuple-element.59), channel_id=1, source_target_pairs={{0,12},{1,13},{2,14},{3,15},{4,0},{5,1},{6,2},{7,3},{8,4},{9,5},{1... | collective-permute-start | bytes 3145736 | tf_op jit(solution)/shard_map/ppermute | solution.py:421
  48.9 1.3 collective-permute-done.2.rest_3_.rest_4_
  50.2 0.0 copy-done.5
  50.2 1.0 copy-done.6
  51.2 2.7 %broadcast_in_dim.20 = bf16[4,256,1024]{2,1,0:T(8,128)(2,1)} broadcast(bf16[256,1024]{1,0:T(8,128)(2,1)} %bitcast.63), dimensions={1,2} | broadcast | bytes 2621440 | tf_op jit(solution)/shard_map/broadcast_in_dim | solution.py:489
  53.9 5.2 %all-to-all-start.1 = ((bf16[4,256,1024]{2,1,0:T(8,128)(2,1)}), bf16[4,256,1024]{2,1,0:T(8,128)(2,1)S(1)}, u32[]{:S(2)}, u32[]{:S(2)}) async-start(bf16[4,256,1024]{2,1,0:T(8,128)(2,1)} %broadcast_in_dim.20), calls=%async_computation.1 | async-start | bytes 4194304 | tf_op jit(solution)/shard_map/all_to_all | solution.py:490
  59.1 1.6 %collective-permute-start.3 = (bf16[1024,512]{1,0:T(8,128)(2,1)}, bf16[1024,512]{1,0:T(8,128)(2,1)S(1)}, u32[]{:S(2)}, u32[]{:S(2)}) collective-permute-start(bf16[1024,512]{1,0:T(8,128)(2,1)} %copy-done.6), channel_id=1, source_target_pairs={{0,1},{1,2},{2,3},{3,0},{4,5},{5,6},{6,7},{7,4},{8,9},{9,10},{10,1... | collective-permute-start | bytes 3145736 | tf_op jit(solution)/shard_map/ppermute | solution.py:421
  60.6 1.7 %collective-permute-start.4 = (bf16[1024,512]{1,0:T(8,128)(2,1)}, bf16[1024,512]{1,0:T(8,128)(2,1)}, u32[]{:S(2)}, u32[]{:S(2)}) collective-permute-start(bf16[1024,512]{1,0:T(8,128)(2,1)} %copy-done.6), channel_id=1, source_target_pairs={{0,3},{1,0},{2,1},{3,2},{4,7},{5,4},{6,5},{7,6},{8,11},{9,8},{10,9... | collective-permute-start | bytes 3145736 | tf_op jit(solution)/shard_map/ppermute | solution.py:421
  62.3 6.4 %weight_grad_chunks.2 = (f32[1024,512]{1,0:T(8,128)}, f32[1024,512]{1,0:T(8,128)}, f32[1024,512]{1,0:T(8,128)}, f32[1024,512]{1,0:T(8,128)}) custom-call(s32[1]{0:T(128)} %bitcast.39.place_ref, bf16[512,8192]{1,0:T(8,128)(2,1)} %bitcast.52, bf16[512,512]{1,0:T(8,128)(2,1)} %get-tuple-element.49.scaled_ref), custom_call_target="tpu_custom_call" | custom-call | flops 2147483648 | bytes 8388608 | tf_op jit(solution)/shard_map/weight_grad_chunks/pallas_call | solution.py:168
  68.7 2.9 %assemble.3 = (bf16[512,512]{1,0:T(8,128)(2,1)}, bf16[512,512]{1,0:T(8,128)(2,1)}) custom-call(f32[1024,512]{1,0:T(8,128)} %get-tuple-element.53.refs_0_, bf16[1024,512]{1,0:T(8,128)(2,1)} %copy-done.1, bf16[1024,512]{1,0:T(8,128)(2,1)} %copy-done.2), custom_call_target="tpu_custom_call" | custom-call | flops 524288 | bytes 3145728 | tf_op jit(solution)/shard_map/assemble/pallas_call | solution.py:245
  71.6 1.9 %collective-permute-done.9.refs_1_.refs_6_ = bf16[1024,512]{1,0:T(8,128)(2,1)} collective-permute-done((bf16[1024,512]{1,0:T(8,128)(2,1)}, bf16[1024,512]{1,0:T(8,128)(2,1)}, u32[]{:S(2)}, u32[]{:S(2)}) %collective-permute-start.9) | collective-permute-done | bytes 1048608 | tf_op jit(solution)/shard_map/ppermute | solution.py:421
  73.5 3.2 %collective-permute-start.12 = (bf16[512,512]{1,0:T(8,128)(2,1)}, bf16[512,512]{1,0:T(8,128)(2,1)}, u32[]{:S(2)}, u32[]{:S(2)}) collective-permute-start(bf16[512,512]{1,0:T(8,128)(2,1)} %get-tuple-element.61), channel_id=1, source_target_pairs={{0,12},{1,13},{2,14},{3,15},{4,0},{5,1},{6,2},{7,3},{8,4},{9,5},{1... | collective-permute-start | bytes 1572872 | tf_op jit(solution)/shard_map/ppermute | solution.py:421
  76.8 9.3 %collective-permute-done.3.rest_4_.rest_5_ = bf16[1024,512]{1,0:T(8,128)(2,1)S(1)} collective-permute-done((bf16[1024,512]{1,0:T(8,128)(2,1)}, bf16[1024,512]{1,0:T(8,128)(2,1)S(1)}, u32[]{:S(2)}, u32[]{:S(2)}) %collective-permute-start.3) | collective-permute-done | bytes 1048608 | tf_op jit(solution)/shard_map/ppermute | solution.py:421
  86.1 0.1 collective-permute-done.4.rest_5_.rest_6_
  86.2 1.6 %collective-permute-start.5 = (bf16[1024,512]{1,0:T(8,128)(2,1)S(1)}, bf16[1024,512]{1,0:T(8,128)(2,1)}, u32[]{:S(2)}, u32[]{:S(2)}) collective-permute-start(bf16[1024,512]{1,0:T(8,128)(2,1)S(1)} %copy-done.4), channel_id=1, source_target_pairs={{0,1},{1,2},{2,3},{3,0},{4,5},{5,6},{6,7},{7,4},{8,9},{9,10},{10,1... | collective-permute-start | bytes 3145736 | tf_op jit(solution)/shard_map/ppermute | solution.py:421
  87.8 1.7 %collective-permute-start.6 = (bf16[1024,512]{1,0:T(8,128)(2,1)}, bf16[1024,512]{1,0:T(8,128)(2,1)}, u32[]{:S(2)}, u32[]{:S(2)}) collective-permute-start(bf16[1024,512]{1,0:T(8,128)(2,1)} %collective-permute-done.4.rest_5_.rest_6_), channel_id=1, source_target_pairs={{0,3},{1,0},{2,1},{3,2},{4,7},{5,4},{6,5},{7,6},{8,11},{9,8},{10,9... | collective-permute-start | bytes 3145736 | tf_op jit(solution)/shard_map/ppermute | solution.py:421
  89.5 0.6 stack.133.owners_ref
  90.1 2.8 %assemble.4 = (bf16[512,512]{1,0:T(8,128)(2,1)}, bf16[512,512]{1,0:T(8,128)(2,1)}) custom-call(f32[1024,512]{1,0:T(8,128)} %get-tuple-element.63.refs_0_, bf16[1024,512]{1,0:T(8,128)(2,1)} %collective-permute-done.9.refs_1_.refs_6_, bf16[1024,512]{1,0:T(8,128)(2,1)} %collective-permute-done.10.refs_2_.refs_7_), custom_call_target="tpu_custom_call" | custom-call | flops 524288 | bytes 3145728 | tf_op jit(solution)/shard_map/assemble/pallas_call | solution.py:245
  92.9 0.8 collective-permute-start.13
  93.7 2.6 %collective-permute-start.14 = (bf16[512,512]{1,0:T(8,128)(2,1)}, bf16[512,512]{1,0:T(8,128)(2,1)}, u32[]{:S(2)}, u32[]{:S(2)}) collective-permute-start(bf16[512,512]{1,0:T(8,128)(2,1)} %get-tuple-element.67), channel_id=1, source_target_pairs={{0,12},{1,13},{2,14},{3,15},{4,0},{5,1},{6,2},{7,3},{8,4},{9,5},{1... | collective-permute-start | bytes 1572872 | tf_op jit(solution)/shard_map/ppermute | solution.py:421
  96.3 7.5 %projection.1.total_ref = f32[512,512]{1,0:T(8,128)} custom-call(s32[32]{0:T(128)} %stack.133.owners_ref, bf16[512,8192]{1,0:T(8,128)(2,1)} %bitcast.53, bf16[1024,512]{1,0:T(8,128)(2,1)} %bitcast.58, bf16[1024,512]{1,0:T(8,128)(2,1)} %copy-done.3, bf16[1024,512]{1,0:T(8,128)(2,1)} %copy-done.5, bf16[1024,512]{1,0:T(8,128)(2,1)} %copy-done.6, ...), custom_call_target="tpu_custom_call" | custom-call | flops 3221225472 | bytes 12582912 | tf_op jit(solution)/shard_map/projection/pallas_call | solution.py:291
  103.9 0.4 convert_reduce_fusion.1
  104.2 0.8 copy-done.8
  105.0 0.3 copy-done.9
  105.4 0.1 copy-done.10
  105.5 1.9 %fusion.1 = (bf16[256,1024]{1,0:T(8,128)(2,1)}, f32[256,1024]{1,0:T(8,128)}, f32[256,1024]{1,0:T(8,128)}) fusion(bf16[1,256,1024]{2,1,0:T(8,128)(2,1)S(1)} %copy-done.10, f32[256,1024]{1,0:T(8,128)S(1)} %copy-done.8, f32[256,1024]{1,0:T(8,128)S(1)} %convert_reduce_fusion.1, f32[256,1024]{1,0:T(8,128)S(1)} %copy-done.9), kind=kLoop, calls=%fused_computation.4 | loop fusion | flops 3145728 | bytes 6291456 | tf_op jit(solution)/shard_map/convert_element_type | solution.py:496
  107.4 0.5 collective-permute-done.13.refs_8_
  107.9 4.6 %collective-permute-done.5.rest_3_ = bf16[1024,512]{1,0:T(8,128)(2,1)} collective-permute-done((bf16[1024,512]{1,0:T(8,128)(2,1)S(1)}, bf16[1024,512]{1,0:T(8,128)(2,1)}, u32[]{:S(2)}, u32[]{:S(2)}) %collective-permute-start.5) | collective-permute-done | bytes 1048608 | tf_op jit(solution)/shard_map/ppermute | solution.py:421
  112.5 5.2 %assemble.5 = bf16[2048,512]{1,0:T(8,128)(2,1)} custom-call(f32[1024,512]{1,0:T(8,128)} %get-tuple-element.69.refs_0_, bf16[1024,512]{1,0:T(8,128)(2,1)} %copy-done.1, bf16[1024,512]{1,0:T(8,128)(2,1)} %copy-done.2, bf16[512,512]{1,0:T(8,128)(2,1)} %collective-permute-done.11.refs_3_, bf16[512,512]{1,0:T(8,128)(2,1)} %collective-permute-done.12.refs_4_, ...), custom_call_target="tpu_custom_call" | custom-call | flops 1048576 | bytes 6291456 | tf_op jit(solution)/shard_map/assemble/pallas_call | solution.py:245
  117.7 4.9 %all-to-all-start.2 = ((bf16[8,256,512]{2,1,0:T(8,128)(2,1)}), bf16[8,256,512]{2,1,0:T(8,128)(2,1)S(1)}, u32[]{:S(2)}, u32[]{:S(2)}) async-start(bf16[8,256,512]{2,1,0:T(8,128)(2,1)} %bitcast.60), calls=%async_computation.2 | async-start | bytes 4194304 | tf_op jit(solution)/shard_map/all_to_all | solution.py:508
  122.6 0.6 concatenate.11.owners_ref
  123.2 16.2 %values_and_input_grad.1 = (bf16[512,512]{1,0:T(8,128)(2,1)}, bf16[512,8192]{1,0:T(8,128)(2,1)}) custom-call(s32[32]{0:T(128)} %concatenate.11.owners_ref, bf16[512,8192]{1,0:T(8,128)(2,1)} %bitcast.54, bf16[512,512]{1,0:T(8,128)(2,1)} %bitcast.62, f32[512,128]{1,0:T(8,128)} %get-tuple-element.43.inv_ref, f32[512,512]{1,0:T(8,128)} %projection.1.total_ref, ...), custom_call_target="tpu_custom_call" | custom-call | flops 4294967296 | bytes 25165824 | tf_op jit(solution)/shard_map/values_and_input_grad/pallas_call | solution.py:394
  139.5 8.8 %all-to-all-done.2 = bf16[8,256,512]{2,1,0:T(8,128)(2,1)S(1)} async-done(((bf16[8,256,512]{2,1,0:T(8,128)(2,1)}), bf16[8,256,512]{2,1,0:T(8,128)(2,1)S(1)}, u32[]{:S(2)}, u32[]{:S(2)}) %all-to-all-start.2) | async-done | bytes 2097184 | tf_op jit(solution)/shard_map/all_to_all | solution.py:508
  148.3 0.3 convert_reduce_fusion
  148.6 0.9 bitcast_multiply_fusion
  (29 shorter events, 0.1 us)
Async XLA Ops:
  3.4 19.7 %all-to-all-start = ((bf16[4,256,512]{2,1,0:T(8,128)(2,1)}), bf16[4,256,512]{2,1,0:T(8,128)(2,1)S(1)}, u32[]{:S(2)}, u32[]{:S(2)}) async-start(bf16[4,256,512]{2,1,0:T(8,128)(2,1)} %broadcast_in_dim.17), calls=%async_computation | async-start | bytes 2097152 | tf_op jit(solution)/shard_map/all_to_all | solution.py:461
  19.7 26.1 %collective-permute-start.7 = (bf16[1024,512]{1,0:T(8,128)(2,1)}, bf16[1024,512]{1,0:T(8,128)(2,1)S(1)}, u32[]{:S(2)}, u32[]{:S(2)}) collective-permute-start(bf16[1024,512]{1,0:T(8,128)(2,1)} %get-tuple-element.51), channel_id=1, source_target_pairs={{0,4},{1,5},{2,6},{3,7},{4,8},{5,9},{6,10},{7,11},{8,12},{9,13},{1... | collective-permute-start | bytes 3145736 | tf_op jit(solution)/shard_map/ppermute | solution.py:421
  21.8 24.3 %collective-permute-start.8 = (bf16[1024,512]{1,0:T(8,128)(2,1)}, bf16[1024,512]{1,0:T(8,128)(2,1)S(1)}, u32[]{:S(2)}, u32[]{:S(2)}) collective-permute-start(bf16[1024,512]{1,0:T(8,128)(2,1)} %get-tuple-element.52), channel_id=1, source_target_pairs={{0,12},{1,13},{2,14},{3,15},{4,0},{5,1},{6,2},{7,3},{8,4},{9,5},{1... | collective-permute-start | bytes 3145736 | tf_op jit(solution)/shard_map/ppermute | solution.py:421
  23.1 30.8 %copy-start = (bf16[4,256,512]{2,1,0:T(8,128)(2,1)}, bf16[4,256,512]{2,1,0:T(8,128)(2,1)S(1)}, u32[]{:S(2)}) copy-start(bf16[4,256,512]{2,1,0:T(8,128)(2,1)S(1)} %all-to-all-done) | copy-start | bytes 3145732
  23.1 25.8 %collective-permute-start = (bf16[1024,512]{1,0:T(8,128)(2,1)S(1)}, bf16[1024,512]{1,0:T(8,128)(2,1)S(1)}, u32[]{:S(2)}, u32[]{:S(2)}) collective-permute-start(bf16[1024,512]{1,0:T(8,128)(2,1)S(1)} %bitcast.55), channel_id=1, source_target_pairs={{0,1},{1,2},{2,3},{3,0},{4,5},{5,6},{6,7},{7,4},{8,9},{9,10},{10,1... | collective-permute-start | bytes 3145736 | tf_op jit(solution)/shard_map/ppermute | solution.py:421
  24.7 24.2 %collective-permute-start.1 = (bf16[1024,512]{1,0:T(8,128)(2,1)S(1)}, bf16[1024,512]{1,0:T(8,128)(2,1)S(1)}, u32[]{:S(2)}, u32[]{:S(2)}) collective-permute-start(bf16[1024,512]{1,0:T(8,128)(2,1)S(1)} %bitcast.56), channel_id=1, source_target_pairs={{0,3},{1,0},{2,1},{3,2},{4,7},{5,4},{6,5},{7,6},{8,11},{9,8},{10,9... | collective-permute-start | bytes 3145736 | tf_op jit(solution)/shard_map/ppermute | solution.py:421
  26.4 23.8 %collective-permute-start.2 = (bf16[1024,512]{1,0:T(8,128)(2,1)S(1)}, bf16[1024,512]{1,0:T(8,128)(2,1)S(1)}, u32[]{:S(2)}, u32[]{:S(2)}) collective-permute-start(bf16[1024,512]{1,0:T(8,128)(2,1)S(1)} %bitcast.57), channel_id=1, source_target_pairs={{0,16},{1,17},{2,18},{3,19},{4,20},{5,21},{6,22},{7,23},{8,24},{9,... | collective-permute-start | bytes 3145736 | tf_op jit(solution)/shard_map/ppermute | solution.py:421
  45.8 8.0 %copy-start.1 = (bf16[1024,512]{1,0:T(8,128)(2,1)}, bf16[1024,512]{1,0:T(8,128)(2,1)S(1)}, u32[]{:S(2)}) copy-start(bf16[1024,512]{1,0:T(8,128)(2,1)S(1)} %collective-permute-done.7.refs_1_) | copy-start | bytes 3145732
  46.1 7.8 %copy-start.2 = (bf16[1024,512]{1,0:T(8,128)(2,1)}, bf16[1024,512]{1,0:T(8,128)(2,1)S(1)}, u32[]{:S(2)}) copy-start(bf16[1024,512]{1,0:T(8,128)(2,1)S(1)} %collective-permute-done.8.refs_2_) | copy-start | bytes 3145732
  46.1 25.5 %collective-permute-start.10 = (bf16[1024,512]{1,0:T(8,128)(2,1)}, bf16[1024,512]{1,0:T(8,128)(2,1)}, u32[]{:S(2)}, u32[]{:S(2)}) collective-permute-start(bf16[1024,512]{1,0:T(8,128)(2,1)} %get-tuple-element.59), channel_id=1, source_target_pairs={{0,12},{1,13},{2,14},{3,15},{4,0},{5,1},{6,2},{7,3},{8,4},{9,5},{1... | collective-permute-start | bytes 3145736 | tf_op jit(solution)/shard_map/ppermute | solution.py:421
  48.9 24.7 %collective-permute-start.9 = (bf16[1024,512]{1,0:T(8,128)(2,1)}, bf16[1024,512]{1,0:T(8,128)(2,1)}, u32[]{:S(2)}, u32[]{:S(2)}) collective-permute-start(bf16[1024,512]{1,0:T(8,128)(2,1)} %get-tuple-element.58), channel_id=1, source_target_pairs={{0,4},{1,5},{2,6},{3,7},{4,8},{5,9},{6,10},{7,11},{8,12},{9,13},{1... | collective-permute-start | bytes 3145736 | tf_op jit(solution)/shard_map/ppermute | solution.py:421
  48.9 1.3 copy-start.3
  48.9 1.3 copy-start.5
  50.2 1.0 copy-start.6
  53.9 49.9 %all-to-all-start.1 = ((bf16[4,256,1024]{2,1,0:T(8,128)(2,1)}), bf16[4,256,1024]{2,1,0:T(8,128)(2,1)S(1)}, u32[]{:S(2)}, u32[]{:S(2)}) async-start(bf16[4,256,1024]{2,1,0:T(8,128)(2,1)} %broadcast_in_dim.20), calls=%async_computation.1 | async-start | bytes 4194304 | tf_op jit(solution)/shard_map/all_to_all | solution.py:490
  59.1 27.1 %collective-permute-start.3 = (bf16[1024,512]{1,0:T(8,128)(2,1)}, bf16[1024,512]{1,0:T(8,128)(2,1)S(1)}, u32[]{:S(2)}, u32[]{:S(2)}) collective-permute-start(bf16[1024,512]{1,0:T(8,128)(2,1)} %copy-done.6), channel_id=1, source_target_pairs={{0,1},{1,2},{2,3},{3,0},{4,5},{5,6},{6,7},{7,4},{8,9},{9,10},{10,1... | collective-permute-start | bytes 3145736 | tf_op jit(solution)/shard_map/ppermute | solution.py:421
  60.6 25.6 %collective-permute-start.4 = (bf16[1024,512]{1,0:T(8,128)(2,1)}, bf16[1024,512]{1,0:T(8,128)(2,1)}, u32[]{:S(2)}, u32[]{:S(2)}) collective-permute-start(bf16[1024,512]{1,0:T(8,128)(2,1)} %copy-done.6), channel_id=1, source_target_pairs={{0,3},{1,0},{2,1},{3,2},{4,7},{5,4},{6,5},{7,6},{8,11},{9,8},{10,9... | collective-permute-start | bytes 3145736 | tf_op jit(solution)/shard_map/ppermute | solution.py:421
  68.7 17.5 %copy-start.4 = (bf16[1024,512]{1,0:T(8,128)(2,1)S(1)}, bf16[1024,512]{1,0:T(8,128)(2,1)}, u32[]{:S(2)}) copy-start(bf16[1024,512]{1,0:T(8,128)(2,1)} %copy-done.3) | copy-start | bytes 3145732
  73.5 19.4 %collective-permute-start.11 = (bf16[512,512]{1,0:T(8,128)(2,1)}, bf16[512,512]{1,0:T(8,128)(2,1)}, u32[]{:S(2)}, u32[]{:S(2)}) collective-permute-start(bf16[512,512]{1,0:T(8,128)(2,1)} %get-tuple-element.60), channel_id=1, source_target_pairs={{0,4},{1,5},{2,6},{3,7},{4,8},{5,9},{6,10},{7,11},{8,12},{9,13},{1... | collective-permute-start | bytes 1572872 | tf_op jit(solution)/shard_map/ppermute | solution.py:421
  73.5 19.4 %collective-permute-start.12 = (bf16[512,512]{1,0:T(8,128)(2,1)}, bf16[512,512]{1,0:T(8,128)(2,1)}, u32[]{:S(2)}, u32[]{:S(2)}) collective-permute-start(bf16[512,512]{1,0:T(8,128)(2,1)} %get-tuple-element.61), channel_id=1, source_target_pairs={{0,12},{1,13},{2,14},{3,15},{4,0},{5,1},{6,2},{7,3},{8,4},{9,5},{1... | collective-permute-start | bytes 1572872 | tf_op jit(solution)/shard_map/ppermute | solution.py:421
  86.1 1.7 %copy-start.7 = (bf16[1024,512]{1,0:T(8,128)(2,1)}, bf16[1024,512]{1,0:T(8,128)(2,1)S(1)}, u32[]{:S(2)}) copy-start(bf16[1024,512]{1,0:T(8,128)(2,1)S(1)} %collective-permute-done.3.rest_4_.rest_5_) | copy-start | bytes 3145732
  86.2 26.2 %collective-permute-start.5 = (bf16[1024,512]{1,0:T(8,128)(2,1)S(1)}, bf16[1024,512]{1,0:T(8,128)(2,1)}, u32[]{:S(2)}, u32[]{:S(2)}) collective-permute-start(bf16[1024,512]{1,0:T(8,128)(2,1)S(1)} %copy-done.4), channel_id=1, source_target_pairs={{0,1},{1,2},{2,3},{3,0},{4,5},{5,6},{6,7},{7,4},{8,9},{9,10},{10,1... | collective-permute-start | bytes 3145736 | tf_op jit(solution)/shard_map/ppermute | solution.py:421
  87.8 24.7 %collective-permute-start.6 = (bf16[1024,512]{1,0:T(8,128)(2,1)}, bf16[1024,512]{1,0:T(8,128)(2,1)}, u32[]{:S(2)}, u32[]{:S(2)}) collective-permute-start(bf16[1024,512]{1,0:T(8,128)(2,1)} %collective-permute-done.4.rest_5_.rest_6_), channel_id=1, source_target_pairs={{0,3},{1,0},{2,1},{3,2},{4,7},{5,4},{6,5},{7,6},{8,11},{9,8},{10,9... | collective-permute-start | bytes 3145736 | tf_op jit(solution)/shard_map/ppermute | solution.py:421
  92.9 15.0 %collective-permute-start.13 = (bf16[512,512]{1,0:T(8,128)(2,1)}, bf16[512,512]{1,0:T(8,128)(2,1)}, u32[]{:S(2)}, u32[]{:S(2)}) collective-permute-start(bf16[512,512]{1,0:T(8,128)(2,1)} %get-tuple-element.66), channel_id=1, source_target_pairs={{0,4},{1,5},{2,6},{3,7},{4,8},{5,9},{6,10},{7,11},{8,12},{9,13},{1... | collective-permute-start | bytes 1572872 | tf_op jit(solution)/shard_map/ppermute | solution.py:421
  93.7 14.2 %collective-permute-start.14 = (bf16[512,512]{1,0:T(8,128)(2,1)}, bf16[512,512]{1,0:T(8,128)(2,1)}, u32[]{:S(2)}, u32[]{:S(2)}) collective-permute-start(bf16[512,512]{1,0:T(8,128)(2,1)} %get-tuple-element.67), channel_id=1, source_target_pairs={{0,12},{1,13},{2,14},{3,15},{4,0},{5,1},{6,2},{7,3},{8,4},{9,5},{1... | collective-permute-start | bytes 1572872 | tf_op jit(solution)/shard_map/ppermute | solution.py:421
  103.8 1.2 copy-start.8
  103.8 1.5 %copy-start.9 = (f32[256,1024]{1,0:T(8,128)S(1)}, f32[256,1024]{1,0:T(8,128)}, u32[]{:S(2)}) copy-start(f32[256,1024]{1,0:T(8,128)} %param.13) | copy-start | bytes 3145732
  103.8 1.7 %copy-start.10 = (bf16[1,256,1024]{2,1,0:T(8,128)(2,1)S(1)}, bf16[1,256,1024]{2,1,0:T(8,128)(2,1)}, u32[]{:S(2)}) copy-start(bf16[1,256,1024]{2,1,0:T(8,128)(2,1)} %param.15) | copy-start | bytes 1572868
  117.7 30.6 %all-to-all-start.2 = ((bf16[8,256,512]{2,1,0:T(8,128)(2,1)}), bf16[8,256,512]{2,1,0:T(8,128)(2,1)S(1)}, u32[]{:S(2)}, u32[]{:S(2)}) async-start(bf16[8,256,512]{2,1,0:T(8,128)(2,1)} %bitcast.60), calls=%async_computation.2 | async-start | bytes 4194304 | tf_op jit(solution)/shard_map/all_to_all | solution.py:508

commit v3 on v2

--- a/solution.py
+++ b/solution.py
@@ -504,7 +504,7 @@
         for n in (0, 5):
             came = [(n + 2 - z, chunk + start), (n + 3 + z, start)]
             segments.append((half, [(n, k * half), *came]))
-    (ring,) = assemble(after(arrays, far, product, new_local), [segments])
+    (ring,) = assemble(after(arrays, far, product), [segments])
     group = lax.all_to_all(ring.reshape(BLOCKS, rows, kv), "fsdp", 0, 0, axis_index_groups=ZY_GROUPS)
 
     values, input_grad = values_and_input_grad(

time: 151 us -> 140 us (0.927)
  waiting for transfers between devices: 44.4 us -> 33.1 us
  other arithmetic: 5.2 us -> 7.04 us
    ppermute x15, waiting for transfers between devices: 35.6 us -> 29.2 us  [send(): return lax.ppermute(block, 'fsdp', where)]
    all_to_all x1, waiting for transfers between devices: 8.84 us -> 3.87 us  [body(): lax.all_to_all(ring.reshape(BLOCKS, rows, kv), 'fsdp', 0, 0, axis_index_g...]
    broadcast_in_dim x0 -> x1, other arithmetic: none -> 1.89 us  [body(): new_local[None]]
    convert_element_type x1 -> x0, other arithmetic: 1.88 us -> none  [body(): new_local = (merge_weight * frag_local[0].astype(f32) + (1.0 - merge_weig...]
    reduce_sum x1, other arithmetic: 0.38 us -> 2.22 us  [body(): total = jnp.sum(lax.all_to_all(everyone, 'rep', 0, 0).astype(f32), axis=0)]
  transfers between devices with their start and end apart: 18 -> 18, of which waited for: 9 -> 8; matrix products, arithmetic and copies ran while one was open for 4% -> 6% of each run, Pallas kernels for 32% -> 38%
where the time goes in v3:
time: 140 us; the launch traced here: 139 us
  Pallas kernels  53 us (38%)
  starting transfers between devices  38.3 us (27%)
  waiting for transfers between devices  33.1 us (24%)
  other arithmetic  7.04 us (5%)
  local copies, waits for them, and re-layouts  6.4 us (5%)
    ppermute x15, waiting for transfers between devices, send(): return lax.ppermute(block, 'fsdp', where)  29.2 us
    ppermute x15, starting transfers between devices, send(): return lax.ppermute(block, 'fsdp', where)  24.4 us
    pallas_call x1, Pallas kernels, values_and_input_grad(): pl.pallas_call(functools.partial(input_grad_kernel, width, factor, late),...  16.2 us
    pallas_call x2, Pallas kernels, weight_grad_chunks(): pl.pallas_call(functools.partial(weight_grad_kernel, todo), in_specs=[SME...  12.7 us
    pallas_call x3, Pallas kernels, assemble(): pl.pallas_call(functools.partial(assemble_kernel, plan, [a.shape[0] for a...  10.8 us
    pallas_call x1, Pallas kernels, projection(): pl.pallas_call(functools.partial(projection_kernel, count), in_specs=[SME...  7.55 us
    pallas_call x1, Pallas kernels, norm_and_scaled_cotangent(): pl.pallas_call(functools.partial(norm_kernel, width), in_specs=[HBM, VMEM...  5.73 us
    all_to_all x1, starting transfers between devices, body(): total = jnp.sum(lax.all_to_all(everyone, 'rep', 0, 0).astype(f32), axis=0)  4.98 us
  transfers between devices with their start and end apart: 18, of which 8 were waited for; matrix products, arithmetic and copies ran while one was open for 6% of the time, Pallas kernels for 38%

profile of v3, /device:TPU:0, one launch (start us, length us, event | category | flops | bytes accessed | tf_op | source)
XLA Modules:
  0.0 138.6 jit_solution(1639988608836878299)
XLA Ops:
  0.6 0.7 convert_element_type.48
  1.3 1.1 fusion.3
  2.4 1.1 broadcast_in_dim.17
  3.4 4.4 %all-to-all-start = ((bf16[4,256,512]{2,1,0:T(8,128)(2,1)}), bf16[4,256,512]{2,1,0:T(8,128)(2,1)S(1)}, u32[]{:S(2)}, u32[]{:S(2)}) async-start(bf16[4,256,512]{2,1,0:T(8,128)(2,1)} %broadcast_in_dim.17), calls=%async_computation | async-start | bytes 2097152 | tf_op jit(solution)/shard_map/all_to_all | solution.py:461
  7.8 5.7 %norm_and_scaled_cotangent.1 = (f32[512,128]{1,0:T(8,128)}, bf16[512,512]{1,0:T(8,128)(2,1)}) custom-call(bf16[512,8192]{1,0:T(8,128)(2,1)} %bitcast.51, bf16[512,512]{1,0:T(8,128)(2,1)} %bitcast.62), custom_call_target="tpu_custom_call" | custom-call | flops 33554432 | bytes 8388608 | tf_op jit(solution)/shard_map/norm_and_scaled_cotangent/pallas_call | solution.py:108
  13.5 6.2 %weight_grad_chunks.3 = (bf16[1024,512]{1,0:T(8,128)(2,1)}, bf16[1024,512]{1,0:T(8,128)(2,1)}, bf16[1024,512]{1,0:T(8,128)(2,1)}, bf16[1024,512]{1,0:T(8,128)(2,1)}) custom-call(s32[1]{0:T(128)} %bitcast.39.place_ref, bf16[512,8192]{1,0:T(8,128)(2,1)} %bitcast.52, bf16[512,512]{1,0:T(8,128)(2,1)} %get-tuple-element.49.scaled_ref), custom_call_target="tpu_custom_call" | custom-call | flops 2147483648 | bytes 8388608 | tf_op jit(solution)/shard_map/weight_grad_chunks/pallas_call | solution.py:168
  19.7 2.1 %collective-permute-start.7 = (bf16[1024,512]{1,0:T(8,128)(2,1)}, bf16[1024,512]{1,0:T(8,128)(2,1)S(1)}, u32[]{:S(2)}, u32[]{:S(2)}) collective-permute-start(bf16[1024,512]{1,0:T(8,128)(2,1)} %get-tuple-element.51), channel_id=1, source_target_pairs={{0,4},{1,5},{2,6},{3,7},{4,8},{5,9},{6,10},{7,11},{8,12},{9,13},{1... | collective-permute-start | bytes 3145736 | tf_op jit(solution)/shard_map/ppermute | solution.py:421
  21.8 1.3 collective-permute-start.8
  23.1 0.0 all-to-all-done
  23.1 1.6 %collective-permute-start = (bf16[1024,512]{1,0:T(8,128)(2,1)S(1)}, bf16[1024,512]{1,0:T(8,128)(2,1)S(1)}, u32[]{:S(2)}, u32[]{:S(2)}) collective-permute-start(bf16[1024,512]{1,0:T(8,128)(2,1)S(1)} %bitcast.56), channel_id=1, source_target_pairs={{0,1},{1,2},{2,3},{3,0},{4,5},{5,6},{6,7},{7,4},{8,9},{9,10},{10,1... | collective-permute-start | bytes 3145736 | tf_op jit(solution)/shard_map/ppermute | solution.py:421
  24.7 1.7 %collective-permute-start.1 = (bf16[1024,512]{1,0:T(8,128)(2,1)S(1)}, bf16[1024,512]{1,0:T(8,128)(2,1)S(1)}, u32[]{:S(2)}, u32[]{:S(2)}) collective-permute-start(bf16[1024,512]{1,0:T(8,128)(2,1)S(1)} %bitcast.57), channel_id=1, source_target_pairs={{0,3},{1,0},{2,1},{3,2},{4,7},{5,4},{6,5},{7,6},{8,11},{9,8},{10,9... | collective-permute-start | bytes 3145736 | tf_op jit(solution)/shard_map/ppermute | solution.py:421
  26.4 1.9 %collective-permute-start.2 = (bf16[1024,512]{1,0:T(8,128)(2,1)S(1)}, bf16[1024,512]{1,0:T(8,128)(2,1)}, u32[]{:S(2)}, u32[]{:S(2)}) collective-permute-start(bf16[1024,512]{1,0:T(8,128)(2,1)S(1)} %bitcast.58), channel_id=1, source_target_pairs={{0,16},{1,17},{2,18},{3,19},{4,20},{5,21},{6,22},{7,23},{8,24},{9,... | collective-permute-start | bytes 3145736 | tf_op jit(solution)/shard_map/ppermute | solution.py:421
  28.3 17.6 %collective-permute-done.7.refs_1_ = bf16[1024,512]{1,0:T(8,128)(2,1)S(1)} collective-permute-done((bf16[1024,512]{1,0:T(8,128)(2,1)}, bf16[1024,512]{1,0:T(8,128)(2,1)S(1)}, u32[]{:S(2)}, u32[]{:S(2)}) %collective-permute-start.7) | collective-permute-done | bytes 1048608 | tf_op jit(solution)/shard_map/ppermute | solution.py:421
  45.9 0.2 collective-permute-done.8.refs_2_
  46.1 2.8 %collective-permute-start.10 = (bf16[1024,512]{1,0:T(8,128)(2,1)}, bf16[1024,512]{1,0:T(8,128)(2,1)}, u32[]{:S(2)}, u32[]{:S(2)}) collective-permute-start(bf16[1024,512]{1,0:T(8,128)(2,1)} %get-tuple-element.59), channel_id=1, source_target_pairs={{0,12},{1,13},{2,14},{3,15},{4,0},{5,1},{6,2},{7,3},{8,4},{9,5},{1... | collective-permute-start | bytes 3145736 | tf_op jit(solution)/shard_map/ppermute | solution.py:421
  48.9 0.0 collective-permute-done.rest_1_
  48.9 0.0 collective-permute-done.1.rest_2_
  48.9 1.4 collective-permute-done.2.rest_3_.rest_4_
  50.3 1.2 collective-permute-start.3
  51.5 2.1 %collective-permute-start.4 = (bf16[1024,512]{1,0:T(8,128)(2,1)}, bf16[1024,512]{1,0:T(8,128)(2,1)}, u32[]{:S(2)}, u32[]{:S(2)}) collective-permute-start(bf16[1024,512]{1,0:T(8,128)(2,1)} %collective-permute-done.2.rest_3_.rest_4_), channel_id=1, source_target_pairs={{0,3},{1,0},{2,1},{3,2},{4,7},{5,4},{6,5},{7,6},{8,11},{9,8},{10,9... | collective-permute-start | bytes 3145736 | tf_op jit(solution)/shard_map/ppermute | solution.py:421
  53.5 2.7 %broadcast_in_dim.20 = bf16[4,256,1024]{2,1,0:T(8,128)(2,1)} broadcast(bf16[256,1024]{1,0:T(8,128)(2,1)} %bitcast.64), dimensions={1,2} | broadcast | bytes 2621440 | tf_op jit(solution)/shard_map/broadcast_in_dim | solution.py:489
  56.2 5.0 %all-to-all-start.2 = ((bf16[4,256,1024]{2,1,0:T(8,128)(2,1)}), bf16[4,256,1024]{2,1,0:T(8,128)(2,1)S(1)}, u32[]{:S(2)}, u32[]{:S(2)}) async-start(bf16[4,256,1024]{2,1,0:T(8,128)(2,1)} %broadcast_in_dim.20), calls=%async_computation.2 | async-start | bytes 4194304 | tf_op jit(solution)/shard_map/all_to_all | solution.py:490
  61.2 6.5 %weight_grad_chunks.2 = (f32[1024,512]{1,0:T(8,128)}, f32[1024,512]{1,0:T(8,128)}, f32[1024,512]{1,0:T(8,128)}, f32[1024,512]{1,0:T(8,128)}) custom-call(s32[1]{0:T(128)} %bitcast.39.place_ref, bf16[512,8192]{1,0:T(8,128)(2,1)} %bitcast.53, bf16[512,512]{1,0:T(8,128)(2,1)} %get-tuple-element.49.scaled_ref), custom_call_target="tpu_custom_call" | custom-call | flops 2147483648 | bytes 8388608 | tf_op jit(solution)/shard_map/weight_grad_chunks/pallas_call | solution.py:168
  67.7 2.9 %assemble.3 = (bf16[512,512]{1,0:T(8,128)(2,1)}, bf16[512,512]{1,0:T(8,128)(2,1)}) custom-call(f32[1024,512]{1,0:T(8,128)} %get-tuple-element.53.refs_0_, bf16[1024,512]{1,0:T(8,128)(2,1)} %copy-done.2, bf16[1024,512]{1,0:T(8,128)(2,1)} %copy-done.3), custom_call_target="tpu_custom_call" | custom-call | flops 524288 | bytes 3145728 | tf_op jit(solution)/shard_map/assemble/pallas_call | solution.py:245
  70.6 0.0 collective-permute-done.10.refs_2_.refs_7_
  70.6 3.0 %collective-permute-done.9.refs_1_.refs_6_ = bf16[1024,512]{1,0:T(8,128)(2,1)} collective-permute-done((bf16[1024,512]{1,0:T(8,128)(2,1)}, bf16[1024,512]{1,0:T(8,128)(2,1)}, u32[]{:S(2)}, u32[]{:S(2)}) %collective-permute-start.9) | collective-permute-done | bytes 1048608 | tf_op jit(solution)/shard_map/ppermute | solution.py:421
  73.5 3.2 %collective-permute-start.12 = (bf16[512,512]{1,0:T(8,128)(2,1)}, bf16[512,512]{1,0:T(8,128)(2,1)}, u32[]{:S(2)}, u32[]{:S(2)}) collective-permute-start(bf16[512,512]{1,0:T(8,128)(2,1)} %get-tuple-element.61), channel_id=1, source_target_pairs={{0,12},{1,13},{2,14},{3,15},{4,0},{5,1},{6,2},{7,3},{8,4},{9,5},{1... | collective-permute-start | bytes 1572872 | tf_op jit(solution)/shard_map/ppermute | solution.py:421
  76.8 1.7 %collective-permute-start.5 = (bf16[1024,512]{1,0:T(8,128)(2,1)S(1)}, bf16[1024,512]{1,0:T(8,128)(2,1)}, u32[]{:S(2)}, u32[]{:S(2)}) collective-permute-start(bf16[1024,512]{1,0:T(8,128)(2,1)S(1)} %copy-done.5), channel_id=1, source_target_pairs={{0,1},{1,2},{2,3},{3,0},{4,5},{5,6},{6,7},{7,4},{8,9},{9,10},{10,1... | collective-permute-start | bytes 3145736 | tf_op jit(solution)/shard_map/ppermute | solution.py:421
  78.4 1.7 %collective-permute-start.6 = (bf16[1024,512]{1,0:T(8,128)(2,1)}, bf16[1024,512]{1,0:T(8,128)(2,1)}, u32[]{:S(2)}, u32[]{:S(2)}) collective-permute-start(bf16[1024,512]{1,0:T(8,128)(2,1)} %collective-permute-done.4.rest_5_.rest_6_), channel_id=1, source_target_pairs={{0,3},{1,0},{2,1},{3,2},{4,7},{5,4},{6,5},{7,6},{8,11},{9,8},{10,9... | collective-permute-start | bytes 3145736 | tf_op jit(solution)/shard_map/ppermute | solution.py:421
  80.1 2.8 %assemble.4 = (bf16[512,512]{1,0:T(8,128)(2,1)}, bf16[512,512]{1,0:T(8,128)(2,1)}) custom-call(f32[1024,512]{1,0:T(8,128)} %get-tuple-element.63.refs_0_, bf16[1024,512]{1,0:T(8,128)(2,1)} %collective-permute-done.9.refs_1_.refs_6_, bf16[1024,512]{1,0:T(8,128)(2,1)} %collective-permute-done.10.refs_2_.refs_7_), custom_call_target="tpu_custom_call" | custom-call | flops 524288 | bytes 3145728 | tf_op jit(solution)/shard_map/assemble/pallas_call | solution.py:245
  82.9 3.8 %collective-permute-done.11.refs_3_ = bf16[512,512]{1,0:T(8,128)(2,1)} collective-permute-done((bf16[512,512]{1,0:T(8,128)(2,1)}, bf16[512,512]{1,0:T(8,128)(2,1)}, u32[]{:S(2)}, u32[]{:S(2)}) %collective-permute-start.11) | collective-permute-done | bytes 524320 | tf_op jit(solution)/shard_map/ppermute | solution.py:421
  86.7 1.1 collective-permute-start.13
  87.9 2.1 %collective-permute-start.14 = (bf16[512,512]{1,0:T(8,128)(2,1)}, bf16[512,512]{1,0:T(8,128)(2,1)}, u32[]{:S(2)}, u32[]{:S(2)}) collective-permute-start(bf16[512,512]{1,0:T(8,128)(2,1)} %get-tuple-element.67), channel_id=1, source_target_pairs={{0,12},{1,13},{2,14},{3,15},{4,0},{5,1},{6,2},{7,3},{8,4},{9,5},{1... | collective-permute-start | bytes 1572872 | tf_op jit(solution)/shard_map/ppermute | solution.py:421
  90.0 0.7 stack.133.owners_ref
  90.7 7.6 %projection.1.total_ref = f32[512,512]{1,0:T(8,128)} custom-call(s32[32]{0:T(128)} %stack.133.owners_ref, bf16[512,8192]{1,0:T(8,128)(2,1)} %bitcast.54, bf16[1024,512]{1,0:T(8,128)(2,1)} %bitcast.59, bf16[1024,512]{1,0:T(8,128)(2,1)} %copy-done.4, bf16[1024,512]{1,0:T(8,128)(2,1)} %copy-done.6, bf16[1024,512]{1,0:T(8,128)(2,1)} %collective-permute-done.2.rest_3_.rest_4_, ...), custom_call_target="tpu_custom_call" | custom-call | flops 3221225472 | bytes 12582912 | tf_op jit(solution)/shard_map/projection/pallas_call | solution.py:291
  98.2 2.4 %collective-permute-done.13.refs_8_ = bf16[512,512]{1,0:T(8,128)(2,1)} collective-permute-done((bf16[512,512]{1,0:T(8,128)(2,1)}, bf16[512,512]{1,0:T(8,128)(2,1)}, u32[]{:S(2)}, u32[]{:S(2)}) %collective-permute-start.13) | collective-permute-done | bytes 524320 | tf_op jit(solution)/shard_map/ppermute | solution.py:421
  100.6 0.9 collective-permute-done.14.refs_9_
  101.4 5.2 %assemble.5 = bf16[2048,512]{1,0:T(8,128)(2,1)} custom-call(f32[1024,512]{1,0:T(8,128)} %get-tuple-element.68.refs_0_, bf16[1024,512]{1,0:T(8,128)(2,1)} %copy-done.2, bf16[1024,512]{1,0:T(8,128)(2,1)} %copy-done.3, bf16[512,512]{1,0:T(8,128)(2,1)} %collective-permute-done.11.refs_3_, bf16[512,512]{1,0:T(8,128)(2,1)} %collective-permute-done.12.refs_4_, ...), custom_call_target="tpu_custom_call" | custom-call | flops 1048576 | bytes 6291456 | tf_op jit(solution)/shard_map/assemble/pallas_call | solution.py:245
  106.6 0.0 copy-start.1
  106.7 1.3 copy-done.1
  108.0 4.5 %all-to-all-start.1 = ((bf16[8,256,512]{2,1,0:T(8,128)(2,1)}), bf16[8,256,512]{2,1,0:T(8,128)(2,1)S(1)}, u32[]{:S(2)}, u32[]{:S(2)}) async-start(bf16[8,256,512]{2,1,0:T(8,128)(2,1)} %bitcast.61), calls=%async_computation.1 | async-start | bytes 4194304 | tf_op jit(solution)/shard_map/all_to_all | solution.py:508
  112.5 0.6 concatenate.11.owners_ref
  113.1 2.2 %convert_reduce_fusion = f32[256,1024]{1,0:T(8,128)S(1)} fusion(bf16[4,256,1024]{2,1,0:T(8,128)(2,1)} %copy-done.1), kind=kLoop, calls=%fused_computation | loop fusion | flops 1835008 | bytes 3145728 | tf_op jit(solution)/shard_map/reduce_sum | solution.py:490
  115.4 1.9 %fusion.2 = (bf16[1,256,1024]{2,1,0:T(8,128)(2,1)}, f32[256,1024]{1,0:T(8,128)}, f32[256,1024]{1,0:T(8,128)}) fusion(bf16[1,256,1024]{2,1,0:T(8,128)(2,1)S(1)} %copy-done.9, f32[256,1024]{1,0:T(8,128)S(1)} %copy-done.7, f32[256,1024]{1,0:T(8,128)S(1)} %convert_reduce_fusion, f32[256,1024]{1,0:T(8,128)S(1)} %copy-done.8), kind=kLoop, calls=%fused_computation.8 | loop fusion | flops 3145728 | bytes 6291456 | tf_op jit(solution)/shard_map/broadcast_in_dim | solution.py:521
  117.3 16.2 %values_and_input_grad.1 = (bf16[512,512]{1,0:T(8,128)(2,1)}, bf16[512,8192]{1,0:T(8,128)(2,1)}) custom-call(s32[32]{0:T(128)} %concatenate.11.owners_ref, bf16[512,8192]{1,0:T(8,128)(2,1)} %bitcast.55, bf16[512,512]{1,0:T(8,128)(2,1)} %bitcast.63, f32[512,128]{1,0:T(8,128)} %get-tuple-element.43.inv_ref, f32[512,512]{1,0:T(8,128)} %projection.1.total_ref, ...), custom_call_target="tpu_custom_call" | custom-call | flops 4294967296 | bytes 25165824 | tf_op jit(solution)/shard_map/values_and_input_grad/pallas_call | solution.py:394
  133.5 3.9 %all-to-all-done.1 = bf16[8,256,512]{2,1,0:T(8,128)(2,1)S(1)} async-done(((bf16[8,256,512]{2,1,0:T(8,128)(2,1)}), bf16[8,256,512]{2,1,0:T(8,128)(2,1)S(1)}, u32[]{:S(2)}, u32[]{:S(2)}) %all-to-all-start.1) | async-done | bytes 2097184 | tf_op jit(solution)/shard_map/all_to_all | solution.py:508
  137.4 0.3 convert_reduce_fusion.1
  137.7 0.9 bitcast_multiply_fusion
  (27 shorter events, 0.1 us)
Async XLA Ops:
  3.4 19.7 %all-to-all-start = ((bf16[4,256,512]{2,1,0:T(8,128)(2,1)}), bf16[4,256,512]{2,1,0:T(8,128)(2,1)S(1)}, u32[]{:S(2)}, u32[]{:S(2)}) async-start(bf16[4,256,512]{2,1,0:T(8,128)(2,1)} %broadcast_in_dim.17), calls=%async_computation | async-start | bytes 2097152 | tf_op jit(solution)/shard_map/all_to_all | solution.py:461
  19.7 26.1 %collective-permute-start.7 = (bf16[1024,512]{1,0:T(8,128)(2,1)}, bf16[1024,512]{1,0:T(8,128)(2,1)S(1)}, u32[]{:S(2)}, u32[]{:S(2)}) collective-permute-start(bf16[1024,512]{1,0:T(8,128)(2,1)} %get-tuple-element.51), channel_id=1, source_target_pairs={{0,4},{1,5},{2,6},{3,7},{4,8},{5,9},{6,10},{7,11},{8,12},{9,13},{1... | collective-permute-start | bytes 3145736 | tf_op jit(solution)/shard_map/ppermute | solution.py:421
  21.8 24.3 %collective-permute-start.8 = (bf16[1024,512]{1,0:T(8,128)(2,1)}, bf16[1024,512]{1,0:T(8,128)(2,1)S(1)}, u32[]{:S(2)}, u32[]{:S(2)}) collective-permute-start(bf16[1024,512]{1,0:T(8,128)(2,1)} %get-tuple-element.52), channel_id=1, source_target_pairs={{0,12},{1,13},{2,14},{3,15},{4,0},{5,1},{6,2},{7,3},{8,4},{9,5},{1... | collective-permute-start | bytes 3145736 | tf_op jit(solution)/shard_map/ppermute | solution.py:421
  23.1 33.1 %copy-start = (bf16[4,256,512]{2,1,0:T(8,128)(2,1)}, bf16[4,256,512]{2,1,0:T(8,128)(2,1)S(1)}, u32[]{:S(2)}) copy-start(bf16[4,256,512]{2,1,0:T(8,128)(2,1)S(1)} %all-to-all-done) | copy-start | bytes 3145732
  23.1 25.8 %collective-permute-start = (bf16[1024,512]{1,0:T(8,128)(2,1)S(1)}, bf16[1024,512]{1,0:T(8,128)(2,1)S(1)}, u32[]{:S(2)}, u32[]{:S(2)}) collective-permute-start(bf16[1024,512]{1,0:T(8,128)(2,1)S(1)} %bitcast.56), channel_id=1, source_target_pairs={{0,1},{1,2},{2,3},{3,0},{4,5},{5,6},{6,7},{7,4},{8,9},{9,10},{10,1... | collective-permute-start | bytes 3145736 | tf_op jit(solution)/shard_map/ppermute | solution.py:421
  24.7 24.2 %collective-permute-start.1 = (bf16[1024,512]{1,0:T(8,128)(2,1)S(1)}, bf16[1024,512]{1,0:T(8,128)(2,1)S(1)}, u32[]{:S(2)}, u32[]{:S(2)}) collective-permute-start(bf16[1024,512]{1,0:T(8,128)(2,1)S(1)} %bitcast.57), channel_id=1, source_target_pairs={{0,3},{1,0},{2,1},{3,2},{4,7},{5,4},{6,5},{7,6},{8,11},{9,8},{10,9... | collective-permute-start | bytes 3145736 | tf_op jit(solution)/shard_map/ppermute | solution.py:421
  26.4 23.9 %collective-permute-start.2 = (bf16[1024,512]{1,0:T(8,128)(2,1)S(1)}, bf16[1024,512]{1,0:T(8,128)(2,1)}, u32[]{:S(2)}, u32[]{:S(2)}) collective-permute-start(bf16[1024,512]{1,0:T(8,128)(2,1)S(1)} %bitcast.58), channel_id=1, source_target_pairs={{0,16},{1,17},{2,18},{3,19},{4,20},{5,21},{6,22},{7,23},{8,24},{9,... | collective-permute-start | bytes 3145736 | tf_op jit(solution)/shard_map/ppermute | solution.py:421
  45.8 10.3 %copy-start.2 = (bf16[1024,512]{1,0:T(8,128)(2,1)}, bf16[1024,512]{1,0:T(8,128)(2,1)S(1)}, u32[]{:S(2)}) copy-start(bf16[1024,512]{1,0:T(8,128)(2,1)S(1)} %collective-permute-done.7.refs_1_) | copy-start | bytes 3145732
  46.1 10.1 %copy-start.3 = (bf16[1024,512]{1,0:T(8,128)(2,1)}, bf16[1024,512]{1,0:T(8,128)(2,1)S(1)}, u32[]{:S(2)}) copy-start(bf16[1024,512]{1,0:T(8,128)(2,1)S(1)} %collective-permute-done.8.refs_2_) | copy-start | bytes 3145732
  46.1 24.5 %collective-permute-start.10 = (bf16[1024,512]{1,0:T(8,128)(2,1)}, bf16[1024,512]{1,0:T(8,128)(2,1)}, u32[]{:S(2)}, u32[]{:S(2)}) collective-permute-start(bf16[1024,512]{1,0:T(8,128)(2,1)} %get-tuple-element.59), channel_id=1, source_target_pairs={{0,12},{1,13},{2,14},{3,15},{4,0},{5,1},{6,2},{7,3},{8,4},{9,5},{1... | collective-permute-start | bytes 3145736 | tf_op jit(solution)/shard_map/ppermute | solution.py:421
  48.9 24.7 %collective-permute-start.9 = (bf16[1024,512]{1,0:T(8,128)(2,1)}, bf16[1024,512]{1,0:T(8,128)(2,1)}, u32[]{:S(2)}, u32[]{:S(2)}) collective-permute-start(bf16[1024,512]{1,0:T(8,128)(2,1)} %get-tuple-element.58), channel_id=1, source_target_pairs={{0,4},{1,5},{2,6},{3,7},{4,8},{5,9},{6,10},{7,11},{8,12},{9,13},{1... | collective-permute-start | bytes 3145736 | tf_op jit(solution)/shard_map/ppermute | solution.py:421
  48.9 1.4 %copy-start.4 = (bf16[1024,512]{1,0:T(8,128)(2,1)}, bf16[1024,512]{1,0:T(8,128)(2,1)S(1)}, u32[]{:S(2)}) copy-start(bf16[1024,512]{1,0:T(8,128)(2,1)S(1)} %collective-permute-done.rest_1_) | copy-start | bytes 3145732
  48.9 2.6 %copy-start.6 = (bf16[1024,512]{1,0:T(8,128)(2,1)}, bf16[1024,512]{1,0:T(8,128)(2,1)S(1)}, u32[]{:S(2)}) copy-start(bf16[1024,512]{1,0:T(8,128)(2,1)S(1)} %collective-permute-done.1.rest_2_) | copy-start | bytes 3145732
  50.3 26.5 %collective-permute-start.3 = (bf16[1024,512]{1,0:T(8,128)(2,1)}, bf16[1024,512]{1,0:T(8,128)(2,1)}, u32[]{:S(2)}, u32[]{:S(2)}) collective-permute-start(bf16[1024,512]{1,0:T(8,128)(2,1)} %collective-permute-done.2.rest_3_.rest_4_), channel_id=1, source_target_pairs={{0,1},{1,2},{2,3},{3,0},{4,5},{5,6},{6,7},{7,4},{8,9},{9,10},{10,1... | collective-permute-start | bytes 3145736 | tf_op jit(solution)/shard_map/ppermute | solution.py:421
  51.5 25.3 %collective-permute-start.4 = (bf16[1024,512]{1,0:T(8,128)(2,1)}, bf16[1024,512]{1,0:T(8,128)(2,1)}, u32[]{:S(2)}, u32[]{:S(2)}) collective-permute-start(bf16[1024,512]{1,0:T(8,128)(2,1)} %collective-permute-done.2.rest_3_.rest_4_), channel_id=1, source_target_pairs={{0,3},{1,0},{2,1},{3,2},{4,7},{5,4},{6,5},{7,6},{8,11},{9,8},{10,9... | collective-permute-start | bytes 3145736 | tf_op jit(solution)/shard_map/ppermute | solution.py:421
  56.2 50.4 %all-to-all-start.2 = ((bf16[4,256,1024]{2,1,0:T(8,128)(2,1)}), bf16[4,256,1024]{2,1,0:T(8,128)(2,1)S(1)}, u32[]{:S(2)}, u32[]{:S(2)}) async-start(bf16[4,256,1024]{2,1,0:T(8,128)(2,1)} %broadcast_in_dim.20), calls=%async_computation.2 | async-start | bytes 4194304 | tf_op jit(solution)/shard_map/all_to_all | solution.py:490
  67.7 9.1 %copy-start.5 = (bf16[1024,512]{1,0:T(8,128)(2,1)S(1)}, bf16[1024,512]{1,0:T(8,128)(2,1)}, u32[]{:S(2)}) copy-start(bf16[1024,512]{1,0:T(8,128)(2,1)} %copy-done.4) | copy-start | bytes 3145732
  73.5 13.2 %collective-permute-start.11 = (bf16[512,512]{1,0:T(8,128)(2,1)}, bf16[512,512]{1,0:T(8,128)(2,1)}, u32[]{:S(2)}, u32[]{:S(2)}) collective-permute-start(bf16[512,512]{1,0:T(8,128)(2,1)} %get-tuple-element.60), channel_id=1, source_target_pairs={{0,4},{1,5},{2,6},{3,7},{4,8},{5,9},{6,10},{7,11},{8,12},{9,13},{1... | collective-permute-start | bytes 1572872 | tf_op jit(solution)/shard_map/ppermute | solution.py:421
  73.5 13.2 %collective-permute-start.12 = (bf16[512,512]{1,0:T(8,128)(2,1)}, bf16[512,512]{1,0:T(8,128)(2,1)}, u32[]{:S(2)}, u32[]{:S(2)}) collective-permute-start(bf16[512,512]{1,0:T(8,128)(2,1)} %get-tuple-element.61), channel_id=1, source_target_pairs={{0,12},{1,13},{2,14},{3,15},{4,0},{5,1},{6,2},{7,3},{8,4},{9,5},{1... | collective-permute-start | bytes 1572872 | tf_op jit(solution)/shard_map/ppermute | solution.py:421
  76.8 24.6 %collective-permute-start.5 = (bf16[1024,512]{1,0:T(8,128)(2,1)S(1)}, bf16[1024,512]{1,0:T(8,128)(2,1)}, u32[]{:S(2)}, u32[]{:S(2)}) collective-permute-start(bf16[1024,512]{1,0:T(8,128)(2,1)S(1)} %copy-done.5), channel_id=1, source_target_pairs={{0,1},{1,2},{2,3},{3,0},{4,5},{5,6},{6,7},{7,4},{8,9},{9,10},{10,1... | collective-permute-start | bytes 3145736 | tf_op jit(solution)/shard_map/ppermute | solution.py:421
  78.4 23.0 %collective-permute-start.6 = (bf16[1024,512]{1,0:T(8,128)(2,1)}, bf16[1024,512]{1,0:T(8,128)(2,1)}, u32[]{:S(2)}, u32[]{:S(2)}) collective-permute-start(bf16[1024,512]{1,0:T(8,128)(2,1)} %collective-permute-done.4.rest_5_.rest_6_), channel_id=1, source_target_pairs={{0,3},{1,0},{2,1},{3,2},{4,7},{5,4},{6,5},{7,6},{8,11},{9,8},{10,9... | collective-permute-start | bytes 3145736 | tf_op jit(solution)/shard_map/ppermute | solution.py:421
  86.7 13.9 %collective-permute-start.13 = (bf16[512,512]{1,0:T(8,128)(2,1)}, bf16[512,512]{1,0:T(8,128)(2,1)}, u32[]{:S(2)}, u32[]{:S(2)}) collective-permute-start(bf16[512,512]{1,0:T(8,128)(2,1)} %get-tuple-element.66), channel_id=1, source_target_pairs={{0,4},{1,5},{2,6},{3,7},{4,8},{5,9},{6,10},{7,11},{8,12},{9,13},{1... | collective-permute-start | bytes 1572872 | tf_op jit(solution)/shard_map/ppermute | solution.py:421
  87.9 13.6 %collective-permute-start.14 = (bf16[512,512]{1,0:T(8,128)(2,1)}, bf16[512,512]{1,0:T(8,128)(2,1)}, u32[]{:S(2)}, u32[]{:S(2)}) collective-permute-start(bf16[512,512]{1,0:T(8,128)(2,1)} %get-tuple-element.67), channel_id=1, source_target_pairs={{0,12},{1,13},{2,14},{3,15},{4,0},{5,1},{6,2},{7,3},{8,4},{9,5},{1... | collective-permute-start | bytes 1572872 | tf_op jit(solution)/shard_map/ppermute | solution.py:421
  106.6 1.3 copy-start.1
  108.0 29.4 %all-to-all-start.1 = ((bf16[8,256,512]{2,1,0:T(8,128)(2,1)}), bf16[8,256,512]{2,1,0:T(8,128)(2,1)S(1)}, u32[]{:S(2)}, u32[]{:S(2)}) async-start(bf16[8,256,512]{2,1,0:T(8,128)(2,1)} %bitcast.61), calls=%async_computation.1 | async-start | bytes 4194304 | tf_op jit(solution)/shard_map/all_to_all | solution.py:508
  112.5 2.9 %copy-start.7 = (f32[256,1024]{1,0:T(8,128)S(1)}, f32[256,1024]{1,0:T(8,128)}, u32[]{:S(2)}) copy-start(f32[256,1024]{1,0:T(8,128)} %param.12) | copy-start | bytes 3145732
  113.1 2.2 %copy-start.8 = (f32[256,1024]{1,0:T(8,128)S(1)}, f32[256,1024]{1,0:T(8,128)}, u32[]{:S(2)}) copy-start(f32[256,1024]{1,0:T(8,128)} %param.13) | copy-start | bytes 3145732
  113.1 2.2 %copy-start.9 = (bf16[1,256,1024]{2,1,0:T(8,128)(2,1)S(1)}, bf16[1,256,1024]{2,1,0:T(8,128)(2,1)}, u32[]{:S(2)}) copy-start(bf16[1,256,1024]{2,1,0:T(8,128)(2,1)} %param.15) | copy-start | bytes 1572868

commit v4 on v3

--- a/solution.py
+++ b/solution.py
@@ -75,11 +75,19 @@
 REST = ((1, 0), (NX - 1, 1), (0, 0), (0, 1))
 
 
-def norm_kernel(width, x_ref, cot_ref, inv_ref, scaled_ref, held, sems):
+def first_kernel(width, todo, place_ref, x_ref, cot_ref, inv_ref, scaled_ref, *rest):
+    outs, (held, stage, sems, store_sems) = rest[:4], rest[4:]
     chunks, rows = held.shape[:2]
+    cols = width // BLOCKS
+    part = cols // NY // 2
 
     def copy(k):
         return pltpu.make_async_copy(x_ref.at[pl.ds(k * rows, rows)], held.at[k], sems.at[k])
+
+    def store(half, k):
+        n = half * len(todo) + k
+        where = outs[n // 2].at[pl.ds((n % 2) * NY * part, NY * part)]
+        return pltpu.make_async_copy(stage.at[n], where, store_sems.at[n])
 
     for k in range(chunks):
         copy(k).start()
@@ -101,28 +109,49 @@
         inv_ref[here, :] = jnp.broadcast_to(inv, (rows, 128))
         scaled_ref[here, :] = (cot_ref[here, :].astype(jnp.float32) * inv).astype(jnp.bfloat16)
 
-
-def norm_and_scaled_cotangent(x, cot):
+    for k, (d, z) in enumerate(todo):
+        j = z * NX + lax.rem(place_ref[0] + d, NX)
+        for half in (0, 1):
+            for p in range(NY):
+                start = pl.multiple_of(j * cols + (2 * p + half) * part, part)
+                piece = held[:, :, pl.ds(start, part)].reshape(chunks * rows, part)
+                stage[half * len(todo) + k, p * part : (p + 1) * part, :] = lax.dot_general(
+                    piece,
+                    scaled_ref[...],
+                    (((0,), (0,)), ((), ())),
+                    preferred_element_type=jnp.float32,
+                ).astype(stage.dtype)
+            store(half, k).start()
+    for k in range(len(todo)):
+        for half in (0, 1):
+            store(half, k).wait()
+
+
+def norm_and_first_chunks(x, cot, place):
     tokens, width = x.shape
     kv = cot.shape[1]
+    part = width // BLOCKS // NY // 2
     return pl.pallas_call(
-        functools.partial(norm_kernel, width),
-        in_specs=[HBM, VMEM],
-        out_specs=[VMEM, VMEM],
+        functools.partial(first_kernel, width, FIRST),
+        in_specs=[SMEM, HBM, VMEM],
+        out_specs=[VMEM, VMEM] + [HBM] * 4,
         out_shape=[
             jax.ShapeDtypeStruct((tokens, 128), jnp.float32),
             jax.ShapeDtypeStruct((tokens, kv), jnp.bfloat16),
-        ],
+        ]
+        + [jax.ShapeDtypeStruct((2 * NY * part, kv), jnp.bfloat16)] * 4,
         scratch_shapes=[
             pltpu.VMEM((CHUNKS, tokens // CHUNKS, width), jnp.bfloat16),
+            pltpu.VMEM((2 * len(FIRST), NY * part, kv), jnp.bfloat16),
             pltpu.SemaphoreType.DMA((CHUNKS,)),
+            pltpu.SemaphoreType.DMA((2 * len(FIRST),)),
         ],
         compiler_params=pltpu.CompilerParams(vmem_limit_bytes=VMEM_LIMIT),
         cost_estimate=pl.CostEstimate(
-            flops=8 * tokens * width, bytes_accessed=2 * tokens * width, transcendentals=0
-        ),
-        name="norm_and_scaled_cotangent",
-    )(x, cot)
+            flops=tokens * width * kv, bytes_accessed=4 * tokens * width, transcendentals=0
+        ),
+        name="norm_and_first_chunks",
+    )(place, x, cot)
 
 
 def weight_grad_kernel(todo, place_ref, x_ref, scaled_ref, *rest):
@@ -461,10 +490,9 @@
     slab = lax.all_to_all(
         jnp.broadcast_to(own, (NX, rows, kv)), "fsdp", 0, 0, axis_index_groups=X_GROUPS
     ).reshape(NX * rows, kv)
-    inv, scaled = norm_and_scaled_cotangent(x, cot)
+    inv, scaled, *sent = norm_and_first_chunks(x, cot, place)
 
     chunk = NY * half
-    sent = weight_grad_chunks(x, scaled, place, FIRST, jnp.bfloat16)
     got = [[send(sent[0], X_UP), send(sent[1], X_DOWN)]]
     below, above, other = send(slab, Y_UP), send(slab, Y_DOWN), send(slab, Z_SWAP)
 

time: 140 us -> 138 us (0.986)
  Pallas kernels: 53 us -> 50.1 us
    pallas_call x2 -> x1, Pallas kernels: 12.7 us -> 6.5 us  [weight_grad_chunks(): pl.pallas_call(functools.partial(weight_grad_kernel, todo), in_specs=[SME...]
    all_to_all x1, waiting for transfers between devices: 0.01 us -> 3.78 us  [body(): lax.all_to_all(jnp.broadcast_to(own, (NX, rows, kv)), 'fsdp', 0, 0, axis_...]
    pallas_call x1, Pallas kernels: 5.73 us -> 9.07 us  [norm_and_first_chunks(): pl.pallas_call(functools.partial(first_kernel, width, FIRST), in_specs=[S...]
    ppermute x15, waiting for transfers between devices: 29.2 us -> 27.3 us  [send(): return lax.ppermute(block, 'fsdp', where)]
    all_to_all x1, waiting for transfers between devices: 3.87 us -> 2.41 us  [body(): lax.all_to_all(ring.reshape(BLOCKS, rows, kv), 'fsdp', 0, 0, axis_index_g...]
  transfers between devices with their start and end apart: 18 -> 18, of which waited for: 8 -> 10; matrix products, arithmetic and copies ran while one was open for 6% -> 6% of each run, Pallas kernels for 38% -> 37%
where the time goes in v4:
time: 138 us; the launch traced here: 136 us
  Pallas kernels  50.1 us (36%)
  starting transfers between devices  38.6 us (28%)
  waiting for transfers between devices  33.5 us (24%)
  other arithmetic  7.04 us (5%)
  local copies, waits for them, and re-layouts  6.41 us (5%)
    ppermute x15, waiting for transfers between devices, send(): return lax.ppermute(block, 'fsdp', where)  27.3 us
    ppermute x15, starting transfers between devices, send(): return lax.ppermute(block, 'fsdp', where)  23.6 us
    pallas_call x1, Pallas kernels, values_and_input_grad(): pl.pallas_call(functools.partial(input_grad_kernel, width, factor, late),...  16.2 us
    pallas_call x3, Pallas kernels, assemble(): pl.pallas_call(functools.partial(assemble_kernel, plan, [a.shape[0] for a...  10.8 us
    pallas_call x1, Pallas kernels, norm_and_first_chunks(): pl.pallas_call(functools.partial(first_kernel, width, FIRST), in_specs=[S...  9.07 us
    pallas_call x1, Pallas kernels, projection(): pl.pallas_call(functools.partial(projection_kernel, count), in_specs=[SME...  7.55 us
    pallas_call x1, Pallas kernels, weight_grad_chunks(): pl.pallas_call(functools.partial(weight_grad_kernel, todo), in_specs=[SME...  6.5 us
    all_to_all x1, starting transfers between devices, body(): lax.all_to_all(ring.reshape(BLOCKS, rows, kv), 'fsdp', 0, 0, axis_index_g...  5.61 us
  transfers between devices with their start and end apart: 18, of which 10 were waited for; matrix products, arithmetic and copies ran while one was open for 6% of the time, Pallas kernels for 37%

profile of v4, /device:TPU:0, one launch (start us, length us, event | category | flops | bytes accessed | tf_op | source)
XLA Modules:
  0.0 136.5 jit_solution(932694105266321299)
XLA Ops:
  0.6 0.7 convert_element_type.48
  1.3 1.1 fusion.3
  2.4 1.1 broadcast_in_dim.17
  3.4 4.4 %all-to-all-start = ((bf16[4,256,512]{2,1,0:T(8,128)(2,1)}), bf16[4,256,512]{2,1,0:T(8,128)(2,1)S(1)}, u32[]{:S(2)}, u32[]{:S(2)}) async-start(bf16[4,256,512]{2,1,0:T(8,128)(2,1)} %broadcast_in_dim.17), calls=%async_computation | async-start | bytes 2097152 | tf_op jit(solution)/shard_map/all_to_all | solution.py:490
  7.8 9.1 %norm_and_first_chunks.1 = (f32[512,128]{1,0:T(8,128)}, bf16[512,512]{1,0:T(8,128)(2,1)}, bf16[1024,512]{1,0:T(8,128)(2,1)}, bf16[1024,512]{1,0:T(8,128)(2,1)}, ...) custom-call(s32[1]{0:T(128)} %bitcast.34.place_ref, bf16[512,8192]{1,0:T(8,128)(2,1)} %bitcast.51, ...), custom_call_target="tpu_custom_call" | custom-call | flops 2147483648 | bytes 16777216 | tf_op jit(solution)/shard_map/norm_and_first_chunks/pallas_call | solution.py:134
  16.9 2.1 %collective-permute-start.7 = (bf16[1024,512]{1,0:T(8,128)(2,1)}, bf16[1024,512]{1,0:T(8,128)(2,1)S(1)}, u32[]{:S(2)}, u32[]{:S(2)}) collective-permute-start(bf16[1024,512]{1,0:T(8,128)(2,1)} %get-tuple-element.51), channel_id=1, source_target_pairs={{0,4},{1,5},{2,6},{3,7},{4,8},{5,9},{6,10},{7,11},{8,12},{9,13},{1... | collective-permute-start | bytes 3145736 | tf_op jit(solution)/shard_map/ppermute | solution.py:450
  19.0 1.3 collective-permute-start.8
  20.3 3.8 %all-to-all-done = bf16[4,256,512]{2,1,0:T(8,128)(2,1)S(1)} async-done(((bf16[4,256,512]{2,1,0:T(8,128)(2,1)}), bf16[4,256,512]{2,1,0:T(8,128)(2,1)S(1)}, u32[]{:S(2)}, u32[]{:S(2)}) %all-to-all-start) | async-done | bytes 1048608 | tf_op jit(solution)/shard_map/all_to_all | solution.py:490
  24.0 1.6 %collective-permute-start = (bf16[1024,512]{1,0:T(8,128)(2,1)S(1)}, bf16[1024,512]{1,0:T(8,128)(2,1)S(1)}, u32[]{:S(2)}, u32[]{:S(2)}) collective-permute-start(bf16[1024,512]{1,0:T(8,128)(2,1)S(1)} %bitcast.55), channel_id=1, source_target_pairs={{0,1},{1,2},{2,3},{3,0},{4,5},{5,6},{6,7},{7,4},{8,9},{9,10},{10,1... | collective-permute-start | bytes 3145736 | tf_op jit(solution)/shard_map/ppermute | solution.py:450
  25.6 1.7 %collective-permute-start.1 = (bf16[1024,512]{1,0:T(8,128)(2,1)S(1)}, bf16[1024,512]{1,0:T(8,128)(2,1)S(1)}, u32[]{:S(2)}, u32[]{:S(2)}) collective-permute-start(bf16[1024,512]{1,0:T(8,128)(2,1)S(1)} %bitcast.56), channel_id=1, source_target_pairs={{0,3},{1,0},{2,1},{3,2},{4,7},{5,4},{6,5},{7,6},{8,11},{9,8},{10,9... | collective-permute-start | bytes 3145736 | tf_op jit(solution)/shard_map/ppermute | solution.py:450
  27.3 1.9 %collective-permute-start.2 = (bf16[1024,512]{1,0:T(8,128)(2,1)S(1)}, bf16[1024,512]{1,0:T(8,128)(2,1)}, u32[]{:S(2)}, u32[]{:S(2)}) collective-permute-start(bf16[1024,512]{1,0:T(8,128)(2,1)S(1)} %bitcast.57), channel_id=1, source_target_pairs={{0,16},{1,17},{2,18},{3,19},{4,20},{5,21},{6,22},{7,23},{8,24},{9,... | collective-permute-start | bytes 3145736 | tf_op jit(solution)/shard_map/ppermute | solution.py:450
  29.2 16.2 %collective-permute-done.7.refs_1_ = bf16[1024,512]{1,0:T(8,128)(2,1)S(1)} collective-permute-done((bf16[1024,512]{1,0:T(8,128)(2,1)}, bf16[1024,512]{1,0:T(8,128)(2,1)S(1)}, u32[]{:S(2)}, u32[]{:S(2)}) %collective-permute-start.7) | collective-permute-done | bytes 1048608 | tf_op jit(solution)/shard_map/ppermute | solution.py:450
  45.4 1.2 collective-permute-start.10
  46.6 0.9 collective-permute-start.9
  47.5 0.4 collective-permute-done.rest_1_
  47.9 0.0 collective-permute-done.1.rest_2_
  47.9 1.7 %collective-permute-done.2.rest_3_.rest_4_ = bf16[1024,512]{1,0:T(8,128)(2,1)} collective-permute-done((bf16[1024,512]{1,0:T(8,128)(2,1)S(1)}, bf16[1024,512]{1,0:T(8,128)(2,1)}, u32[]{:S(2)}, u32[]{:S(2)}) %collective-permute-start.2) | collective-permute-done | bytes 1048608 | tf_op jit(solution)/shard_map/ppermute | solution.py:450
  49.6 0.4 collective-permute-start.3
  50.0 2.8 %collective-permute-start.4 = (bf16[1024,512]{1,0:T(8,128)(2,1)}, bf16[1024,512]{1,0:T(8,128)(2,1)}, u32[]{:S(2)}, u32[]{:S(2)}) collective-permute-start(bf16[1024,512]{1,0:T(8,128)(2,1)} %collective-permute-done.2.rest_3_.rest_4_), channel_id=1, source_target_pairs={{0,3},{1,0},{2,1},{3,2},{4,7},{5,4},{6,5},{7,6},{8,11},{9,8},{10,9... | collective-permute-start | bytes 3145736 | tf_op jit(solution)/shard_map/ppermute | solution.py:450
  52.9 2.7 %broadcast_in_dim.20 = bf16[4,256,1024]{2,1,0:T(8,128)(2,1)} broadcast(bf16[256,1024]{1,0:T(8,128)(2,1)} %bitcast.63), dimensions={1,2} | broadcast | bytes 2621440 | tf_op jit(solution)/shard_map/broadcast_in_dim | solution.py:517
  55.5 5.0 %all-to-all-start.2 = ((bf16[4,256,1024]{2,1,0:T(8,128)(2,1)}), bf16[4,256,1024]{2,1,0:T(8,128)(2,1)S(1)}, u32[]{:S(2)}, u32[]{:S(2)}) async-start(bf16[4,256,1024]{2,1,0:T(8,128)(2,1)} %broadcast_in_dim.20), calls=%async_computation.2 | async-start | bytes 4194304 | tf_op jit(solution)/shard_map/all_to_all | solution.py:518
  60.5 6.5 %weight_grad_chunks.1 = (f32[1024,512]{1,0:T(8,128)}, f32[1024,512]{1,0:T(8,128)}, f32[1024,512]{1,0:T(8,128)}, f32[1024,512]{1,0:T(8,128)}) custom-call(s32[1]{0:T(128)} %bitcast.34.place_ref, bf16[512,8192]{1,0:T(8,128)(2,1)} %bitcast.52, bf16[512,512]{1,0:T(8,128)(2,1)} %get-tuple-element.49.scaled_ref), custom_call_target="tpu_custom_call" | custom-call | flops 2147483648 | bytes 8388608 | tf_op jit(solution)/shard_map/weight_grad_chunks/pallas_call | solution.py:197
  67.0 2.9 %assemble.3 = (bf16[512,512]{1,0:T(8,128)(2,1)}, bf16[512,512]{1,0:T(8,128)(2,1)}) custom-call(f32[1024,512]{1,0:T(8,128)} %get-tuple-element.53.refs_0_, bf16[1024,512]{1,0:T(8,128)(2,1)} %copy-done.2, bf16[1024,512]{1,0:T(8,128)(2,1)} %copy-done.3), custom_call_target="tpu_custom_call" | custom-call | flops 524288 | bytes 3145728 | tf_op jit(solution)/shard_map/assemble/pallas_call | solution.py:274
  69.9 0.9 collective-permute-done.10.refs_2_.refs_7_
  70.8 1.3 collective-permute-done.9.refs_1_.refs_6_
  72.1 0.5 collective-permute-start.11
  72.6 2.8 %collective-permute-start.12 = (bf16[512,512]{1,0:T(8,128)(2,1)}, bf16[512,512]{1,0:T(8,128)(2,1)}, u32[]{:S(2)}, u32[]{:S(2)}) collective-permute-start(bf16[512,512]{1,0:T(8,128)(2,1)} %get-tuple-element.61), channel_id=1, source_target_pairs={{0,12},{1,13},{2,14},{3,15},{4,0},{5,1},{6,2},{7,3},{8,4},{9,5},{1... | collective-permute-start | bytes 1572872 | tf_op jit(solution)/shard_map/ppermute | solution.py:450
  75.4 1.6 %collective-permute-start.5 = (bf16[1024,512]{1,0:T(8,128)(2,1)S(1)}, bf16[1024,512]{1,0:T(8,128)(2,1)}, u32[]{:S(2)}, u32[]{:S(2)}) collective-permute-start(bf16[1024,512]{1,0:T(8,128)(2,1)S(1)} %copy-done.5), channel_id=1, source_target_pairs={{0,1},{1,2},{2,3},{3,0},{4,5},{5,6},{6,7},{7,4},{8,9},{9,10},{10,1... | collective-permute-start | bytes 3145736 | tf_op jit(solution)/shard_map/ppermute | solution.py:450
  77.0 1.7 %collective-permute-start.6 = (bf16[1024,512]{1,0:T(8,128)(2,1)}, bf16[1024,512]{1,0:T(8,128)(2,1)}, u32[]{:S(2)}, u32[]{:S(2)}) collective-permute-start(bf16[1024,512]{1,0:T(8,128)(2,1)} %collective-permute-done.4.rest_5_.rest_6_), channel_id=1, source_target_pairs={{0,3},{1,0},{2,1},{3,2},{4,7},{5,4},{6,5},{7,6},{8,11},{9,8},{10,9... | collective-permute-start | bytes 3145736 | tf_op jit(solution)/shard_map/ppermute | solution.py:450
  78.7 2.8 %assemble.4 = (bf16[512,512]{1,0:T(8,128)(2,1)}, bf16[512,512]{1,0:T(8,128)(2,1)}) custom-call(f32[1024,512]{1,0:T(8,128)} %get-tuple-element.63.refs_0_, bf16[1024,512]{1,0:T(8,128)(2,1)} %collective-permute-done.9.refs_1_.refs_6_, bf16[1024,512]{1,0:T(8,128)(2,1)} %collective-permute-done.10.refs_2_.refs_7_), custom_call_target="tpu_custom_call" | custom-call | flops 524288 | bytes 3145728 | tf_op jit(solution)/shard_map/assemble/pallas_call | solution.py:274
  81.5 4.4 %collective-permute-done.11.refs_3_ = bf16[512,512]{1,0:T(8,128)(2,1)} collective-permute-done((bf16[512,512]{1,0:T(8,128)(2,1)}, bf16[512,512]{1,0:T(8,128)(2,1)}, u32[]{:S(2)}, u32[]{:S(2)}) %collective-permute-start.11) | collective-permute-done | bytes 524320 | tf_op jit(solution)/shard_map/ppermute | solution.py:450
  85.9 0.0 collective-permute-start.13
  85.9 3.2 %collective-permute-start.14 = (bf16[512,512]{1,0:T(8,128)(2,1)}, bf16[512,512]{1,0:T(8,128)(2,1)}, u32[]{:S(2)}, u32[]{:S(2)}) collective-permute-start(bf16[512,512]{1,0:T(8,128)(2,1)} %get-tuple-element.67), channel_id=1, source_target_pairs={{0,12},{1,13},{2,14},{3,15},{4,0},{5,1},{6,2},{7,3},{8,4},{9,5},{1... | collective-permute-start | bytes 1572872 | tf_op jit(solution)/shard_map/ppermute | solution.py:450
  89.1 0.6 stack.133.owners_ref
  89.7 7.6 %projection.1.total_ref = f32[512,512]{1,0:T(8,128)} custom-call(s32[32]{0:T(128)} %stack.133.owners_ref, bf16[512,8192]{1,0:T(8,128)(2,1)} %bitcast.53, bf16[1024,512]{1,0:T(8,128)(2,1)} %bitcast.58, bf16[1024,512]{1,0:T(8,128)(2,1)} %copy-done.4, bf16[1024,512]{1,0:T(8,128)(2,1)} %copy-done.6, bf16[1024,512]{1,0:T(8,128)(2,1)} %collective-permute-done.2.rest_3_.rest_4_, ...), custom_call_target="tpu_custom_call" | custom-call | flops 3221225472 | bytes 12582912 | tf_op jit(solution)/shard_map/projection/pallas_call | solution.py:320
  97.3 1.4 collective-permute-done.13.refs_8_
  98.7 1.0 collective-permute-done.5.rest_3_
  99.6 5.2 %assemble.5 = bf16[2048,512]{1,0:T(8,128)(2,1)} custom-call(f32[1024,512]{1,0:T(8,128)} %get-tuple-element.68.refs_0_, bf16[1024,512]{1,0:T(8,128)(2,1)} %copy-done.2, bf16[1024,512]{1,0:T(8,128)(2,1)} %copy-done.3, bf16[512,512]{1,0:T(8,128)(2,1)} %collective-permute-done.11.refs_3_, bf16[512,512]{1,0:T(8,128)(2,1)} %collective-permute-done.12.refs_4_, ...), custom_call_target="tpu_custom_call" | custom-call | flops 1048576 | bytes 6291456 | tf_op jit(solution)/shard_map/assemble/pallas_call | solution.py:274
  104.8 0.0 copy-start.1
  104.8 1.3 copy-done.1
  106.2 5.6 %all-to-all-start.1 = ((bf16[8,256,512]{2,1,0:T(8,128)(2,1)}), bf16[8,256,512]{2,1,0:T(8,128)(2,1)S(1)}, u32[]{:S(2)}, u32[]{:S(2)}) async-start(bf16[8,256,512]{2,1,0:T(8,128)(2,1)} %bitcast.60), calls=%async_computation.1 | async-start | bytes 4194304 | tf_op jit(solution)/shard_map/all_to_all | solution.py:536
  111.8 0.7 concatenate.11.owners_ref
  112.5 2.2 %convert_reduce_fusion = f32[256,1024]{1,0:T(8,128)S(1)} fusion(bf16[4,256,1024]{2,1,0:T(8,128)(2,1)} %copy-done.1), kind=kLoop, calls=%fused_computation | loop fusion | flops 1835008 | bytes 3145728 | tf_op jit(solution)/shard_map/reduce_sum | solution.py:518
  114.7 1.9 %fusion.2 = (bf16[1,256,1024]{2,1,0:T(8,128)(2,1)}, f32[256,1024]{1,0:T(8,128)}, f32[256,1024]{1,0:T(8,128)}) fusion(bf16[1,256,1024]{2,1,0:T(8,128)(2,1)S(1)} %copy-done.9, f32[256,1024]{1,0:T(8,128)S(1)} %copy-done.7, f32[256,1024]{1,0:T(8,128)S(1)} %convert_reduce_fusion, f32[256,1024]{1,0:T(8,128)S(1)} %copy-done.8), kind=kLoop, calls=%fused_computation.8 | loop fusion | flops 3145728 | bytes 6291456 | tf_op jit(solution)/shard_map/broadcast_in_dim | solution.py:549
  116.6 16.2 %values_and_input_grad.1 = (bf16[512,512]{1,0:T(8,128)(2,1)}, bf16[512,8192]{1,0:T(8,128)(2,1)}) custom-call(s32[32]{0:T(128)} %concatenate.11.owners_ref, bf16[512,8192]{1,0:T(8,128)(2,1)} %bitcast.54, bf16[512,512]{1,0:T(8,128)(2,1)} %bitcast.62, f32[512,128]{1,0:T(8,128)} %get-tuple-element.43.inv_ref, f32[512,512]{1,0:T(8,128)} %projection.1.total_ref, ...), custom_call_target="tpu_custom_call" | custom-call | flops 4294967296 | bytes 25165824 | tf_op jit(solution)/shard_map/values_and_input_grad/pallas_call | solution.py:423
  132.9 2.4 %all-to-all-done.1 = bf16[8,256,512]{2,1,0:T(8,128)(2,1)S(1)} async-done(((bf16[8,256,512]{2,1,0:T(8,128)(2,1)}), bf16[8,256,512]{2,1,0:T(8,128)(2,1)S(1)}, u32[]{:S(2)}, u32[]{:S(2)}) %all-to-all-start.1) | async-done | bytes 2097184 | tf_op jit(solution)/shard_map/all_to_all | solution.py:536
  135.3 0.3 convert_reduce_fusion.1
  135.6 0.9 bitcast_multiply_fusion
  (26 shorter events, 0.1 us)
Async XLA Ops:
  3.4 20.6 %all-to-all-start = ((bf16[4,256,512]{2,1,0:T(8,128)(2,1)}), bf16[4,256,512]{2,1,0:T(8,128)(2,1)S(1)}, u32[]{:S(2)}, u32[]{:S(2)}) async-start(bf16[4,256,512]{2,1,0:T(8,128)(2,1)} %broadcast_in_dim.17), calls=%async_computation | async-start | bytes 2097152 | tf_op jit(solution)/shard_map/all_to_all | solution.py:490
  16.9 28.5 %collective-permute-start.7 = (bf16[1024,512]{1,0:T(8,128)(2,1)}, bf16[1024,512]{1,0:T(8,128)(2,1)S(1)}, u32[]{:S(2)}, u32[]{:S(2)}) collective-permute-start(bf16[1024,512]{1,0:T(8,128)(2,1)} %get-tuple-element.51), channel_id=1, source_target_pairs={{0,4},{1,5},{2,6},{3,7},{4,8},{5,9},{6,10},{7,11},{8,12},{9,13},{1... | collective-permute-start | bytes 3145736 | tf_op jit(solution)/shard_map/ppermute | solution.py:450
  19.0 26.4 %collective-permute-start.8 = (bf16[1024,512]{1,0:T(8,128)(2,1)}, bf16[1024,512]{1,0:T(8,128)(2,1)S(1)}, u32[]{:S(2)}, u32[]{:S(2)}) collective-permute-start(bf16[1024,512]{1,0:T(8,128)(2,1)} %get-tuple-element.52), channel_id=1, source_target_pairs={{0,12},{1,13},{2,14},{3,15},{4,0},{5,1},{6,2},{7,3},{8,4},{9,5},{1... | collective-permute-start | bytes 3145736 | tf_op jit(solution)/shard_map/ppermute | solution.py:450
  24.0 31.5 %copy-start = (bf16[4,256,512]{2,1,0:T(8,128)(2,1)}, bf16[4,256,512]{2,1,0:T(8,128)(2,1)S(1)}, u32[]{:S(2)}) copy-start(bf16[4,256,512]{2,1,0:T(8,128)(2,1)S(1)} %all-to-all-done) | copy-start | bytes 3145732
  24.0 23.8 %collective-permute-start = (bf16[1024,512]{1,0:T(8,128)(2,1)S(1)}, bf16[1024,512]{1,0:T(8,128)(2,1)S(1)}, u32[]{:S(2)}, u32[]{:S(2)}) collective-permute-start(bf16[1024,512]{1,0:T(8,128)(2,1)S(1)} %bitcast.55), channel_id=1, source_target_pairs={{0,1},{1,2},{2,3},{3,0},{4,5},{5,6},{6,7},{7,4},{8,9},{9,10},{10,1... | collective-permute-start | bytes 3145736 | tf_op jit(solution)/shard_map/ppermute | solution.py:450
  25.6 22.3 %collective-permute-start.1 = (bf16[1024,512]{1,0:T(8,128)(2,1)S(1)}, bf16[1024,512]{1,0:T(8,128)(2,1)S(1)}, u32[]{:S(2)}, u32[]{:S(2)}) collective-permute-start(bf16[1024,512]{1,0:T(8,128)(2,1)S(1)} %bitcast.56), channel_id=1, source_target_pairs={{0,3},{1,0},{2,1},{3,2},{4,7},{5,4},{6,5},{7,6},{8,11},{9,8},{10,9... | collective-permute-start | bytes 3145736 | tf_op jit(solution)/shard_map/ppermute | solution.py:450
  27.3 22.4 %collective-permute-start.2 = (bf16[1024,512]{1,0:T(8,128)(2,1)S(1)}, bf16[1024,512]{1,0:T(8,128)(2,1)}, u32[]{:S(2)}, u32[]{:S(2)}) collective-permute-start(bf16[1024,512]{1,0:T(8,128)(2,1)S(1)} %bitcast.57), channel_id=1, source_target_pairs={{0,16},{1,17},{2,18},{3,19},{4,20},{5,21},{6,22},{7,23},{8,24},{9,... | collective-permute-start | bytes 3145736 | tf_op jit(solution)/shard_map/ppermute | solution.py:450
  45.4 10.2 %copy-start.2 = (bf16[1024,512]{1,0:T(8,128)(2,1)}, bf16[1024,512]{1,0:T(8,128)(2,1)S(1)}, u32[]{:S(2)}) copy-start(bf16[1024,512]{1,0:T(8,128)(2,1)S(1)} %collective-permute-done.7.refs_1_) | copy-start | bytes 3145732
  45.4 10.2 %copy-start.3 = (bf16[1024,512]{1,0:T(8,128)(2,1)}, bf16[1024,512]{1,0:T(8,128)(2,1)S(1)}, u32[]{:S(2)}) copy-start(bf16[1024,512]{1,0:T(8,128)(2,1)S(1)} %collective-permute-done.8.refs_2_) | copy-start | bytes 3145732
  45.4 25.5 %collective-permute-start.10 = (bf16[1024,512]{1,0:T(8,128)(2,1)}, bf16[1024,512]{1,0:T(8,128)(2,1)}, u32[]{:S(2)}, u32[]{:S(2)}) collective-permute-start(bf16[1024,512]{1,0:T(8,128)(2,1)} %get-tuple-element.59), channel_id=1, source_target_pairs={{0,12},{1,13},{2,14},{3,15},{4,0},{5,1},{6,2},{7,3},{8,4},{9,5},{1... | collective-permute-start | bytes 3145736 | tf_op jit(solution)/shard_map/ppermute | solution.py:450
  46.6 25.6 %collective-permute-start.9 = (bf16[1024,512]{1,0:T(8,128)(2,1)}, bf16[1024,512]{1,0:T(8,128)(2,1)}, u32[]{:S(2)}, u32[]{:S(2)}) collective-permute-start(bf16[1024,512]{1,0:T(8,128)(2,1)} %get-tuple-element.58), channel_id=1, source_target_pairs={{0,4},{1,5},{2,6},{3,7},{4,8},{5,9},{6,10},{7,11},{8,12},{9,13},{1... | collective-permute-start | bytes 3145736 | tf_op jit(solution)/shard_map/ppermute | solution.py:450
  47.9 1.7 %copy-start.4 = (bf16[1024,512]{1,0:T(8,128)(2,1)}, bf16[1024,512]{1,0:T(8,128)(2,1)S(1)}, u32[]{:S(2)}) copy-start(bf16[1024,512]{1,0:T(8,128)(2,1)S(1)} %collective-permute-done.rest_1_) | copy-start | bytes 3145732
  47.9 2.1 %copy-start.6 = (bf16[1024,512]{1,0:T(8,128)(2,1)}, bf16[1024,512]{1,0:T(8,128)(2,1)S(1)}, u32[]{:S(2)}) copy-start(bf16[1024,512]{1,0:T(8,128)(2,1)S(1)} %collective-permute-done.1.rest_2_) | copy-start | bytes 3145732
  49.6 25.7 %collective-permute-start.3 = (bf16[1024,512]{1,0:T(8,128)(2,1)}, bf16[1024,512]{1,0:T(8,128)(2,1)}, u32[]{:S(2)}, u32[]{:S(2)}) collective-permute-start(bf16[1024,512]{1,0:T(8,128)(2,1)} %collective-permute-done.2.rest_3_.rest_4_), channel_id=1, source_target_pairs={{0,1},{1,2},{2,3},{3,0},{4,5},{5,6},{6,7},{7,4},{8,9},{9,10},{10,1... | collective-permute-start | bytes 3145736 | tf_op jit(solution)/shard_map/ppermute | solution.py:450
  50.0 25.3 %collective-permute-start.4 = (bf16[1024,512]{1,0:T(8,128)(2,1)}, bf16[1024,512]{1,0:T(8,128)(2,1)}, u32[]{:S(2)}, u32[]{:S(2)}) collective-permute-start(bf16[1024,512]{1,0:T(8,128)(2,1)} %collective-permute-done.2.rest_3_.rest_4_), channel_id=1, source_target_pairs={{0,3},{1,0},{2,1},{3,2},{4,7},{5,4},{6,5},{7,6},{8,11},{9,8},{10,9... | collective-permute-start | bytes 3145736 | tf_op jit(solution)/shard_map/ppermute | solution.py:450
  55.5 49.3 %all-to-all-start.2 = ((bf16[4,256,1024]{2,1,0:T(8,128)(2,1)}), bf16[4,256,1024]{2,1,0:T(8,128)(2,1)S(1)}, u32[]{:S(2)}, u32[]{:S(2)}) async-start(bf16[4,256,1024]{2,1,0:T(8,128)(2,1)} %broadcast_in_dim.20), calls=%async_computation.2 | async-start | bytes 4194304 | tf_op jit(solution)/shard_map/all_to_all | solution.py:518
  67.0 8.3 %copy-start.5 = (bf16[1024,512]{1,0:T(8,128)(2,1)S(1)}, bf16[1024,512]{1,0:T(8,128)(2,1)}, u32[]{:S(2)}) copy-start(bf16[1024,512]{1,0:T(8,128)(2,1)} %copy-done.4) | copy-start | bytes 3145732
  72.1 13.7 %collective-permute-start.11 = (bf16[512,512]{1,0:T(8,128)(2,1)}, bf16[512,512]{1,0:T(8,128)(2,1)}, u32[]{:S(2)}, u32[]{:S(2)}) collective-permute-start(bf16[512,512]{1,0:T(8,128)(2,1)} %get-tuple-element.60), channel_id=1, source_target_pairs={{0,4},{1,5},{2,6},{3,7},{4,8},{5,9},{6,10},{7,11},{8,12},{9,13},{1... | collective-permute-start | bytes 1572872 | tf_op jit(solution)/shard_map/ppermute | solution.py:450
  72.6 13.3 %collective-permute-start.12 = (bf16[512,512]{1,0:T(8,128)(2,1)}, bf16[512,512]{1,0:T(8,128)(2,1)}, u32[]{:S(2)}, u32[]{:S(2)}) collective-permute-start(bf16[512,512]{1,0:T(8,128)(2,1)} %get-tuple-element.61), channel_id=1, source_target_pairs={{0,12},{1,13},{2,14},{3,15},{4,0},{5,1},{6,2},{7,3},{8,4},{9,5},{1... | collective-permute-start | bytes 1572872 | tf_op jit(solution)/shard_map/ppermute | solution.py:450
  75.4 24.3 %collective-permute-start.5 = (bf16[1024,512]{1,0:T(8,128)(2,1)S(1)}, bf16[1024,512]{1,0:T(8,128)(2,1)}, u32[]{:S(2)}, u32[]{:S(2)}) collective-permute-start(bf16[1024,512]{1,0:T(8,128)(2,1)S(1)} %copy-done.5), channel_id=1, source_target_pairs={{0,1},{1,2},{2,3},{3,0},{4,5},{5,6},{6,7},{7,4},{8,9},{9,10},{10,1... | collective-permute-start | bytes 3145736 | tf_op jit(solution)/shard_map/ppermute | solution.py:450
  77.0 22.6 %collective-permute-start.6 = (bf16[1024,512]{1,0:T(8,128)(2,1)}, bf16[1024,512]{1,0:T(8,128)(2,1)}, u32[]{:S(2)}, u32[]{:S(2)}) collective-permute-start(bf16[1024,512]{1,0:T(8,128)(2,1)} %collective-permute-done.4.rest_5_.rest_6_), channel_id=1, source_target_pairs={{0,3},{1,0},{2,1},{3,2},{4,7},{5,4},{6,5},{7,6},{8,11},{9,8},{10,9... | collective-permute-start | bytes 3145736 | tf_op jit(solution)/shard_map/ppermute | solution.py:450
  85.9 12.8 %collective-permute-start.13 = (bf16[512,512]{1,0:T(8,128)(2,1)}, bf16[512,512]{1,0:T(8,128)(2,1)}, u32[]{:S(2)}, u32[]{:S(2)}) collective-permute-start(bf16[512,512]{1,0:T(8,128)(2,1)} %get-tuple-element.66), channel_id=1, source_target_pairs={{0,4},{1,5},{2,6},{3,7},{4,8},{5,9},{6,10},{7,11},{8,12},{9,13},{1... | collective-permute-start | bytes 1572872 | tf_op jit(solution)/shard_map/ppermute | solution.py:450
  85.9 12.8 %collective-permute-start.14 = (bf16[512,512]{1,0:T(8,128)(2,1)}, bf16[512,512]{1,0:T(8,128)(2,1)}, u32[]{:S(2)}, u32[]{:S(2)}) collective-permute-start(bf16[512,512]{1,0:T(8,128)(2,1)} %get-tuple-element.67), channel_id=1, source_target_pairs={{0,12},{1,13},{2,14},{3,15},{4,0},{5,1},{6,2},{7,3},{8,4},{9,5},{1... | collective-permute-start | bytes 1572872 | tf_op jit(solution)/shard_map/ppermute | solution.py:450
  104.8 1.3 copy-start.1
  106.2 29.1 %all-to-all-start.1 = ((bf16[8,256,512]{2,1,0:T(8,128)(2,1)}), bf16[8,256,512]{2,1,0:T(8,128)(2,1)S(1)}, u32[]{:S(2)}, u32[]{:S(2)}) async-start(bf16[8,256,512]{2,1,0:T(8,128)(2,1)} %bitcast.60), calls=%async_computation.1 | async-start | bytes 4194304 | tf_op jit(solution)/shard_map/all_to_all | solution.py:536
  111.8 3.0 %copy-start.7 = (f32[256,1024]{1,0:T(8,128)S(1)}, f32[256,1024]{1,0:T(8,128)}, u32[]{:S(2)}) copy-start(f32[256,1024]{1,0:T(8,128)} %param.12) | copy-start | bytes 3145732
  112.5 2.2 %copy-start.8 = (f32[256,1024]{1,0:T(8,128)S(1)}, f32[256,1024]{1,0:T(8,128)}, u32[]{:S(2)}) copy-start(f32[256,1024]{1,0:T(8,128)} %param.13) | copy-start | bytes 3145732
  112.5 2.2 %copy-start.9 = (bf16[1,256,1024]{2,1,0:T(8,128)(2,1)S(1)}, bf16[1,256,1024]{2,1,0:T(8,128)(2,1)}, u32[]{:S(2)}) copy-start(bf16[1,256,1024]{2,1,0:T(8,128)(2,1)} %param.15) | copy-start | bytes 1572868
